TPU v7x, 256 devices: a whole 4x4x8 slice. The times are simulated.
256 devices in a mesh: sfc: 16 (over x, y), sub: 16 (over z, core).
Axes of the slice: x: 4, y: 4, z: 8, core: 2. Of those that a mesh axis runs over, the one named last changes fastest.
Arguments:
- pot_temp: float32 [8192, 16, 128], P(('sfc', 'sub')), may hold values from -6 to 6
- tracer: float32 [8192, 16, 128], P(('sfc', 'sub')), may hold values from -6 to 6
- wind_u: float32 [8192, 16, 128], P(('sfc', 'sub')), may hold values from -6 to 6
- wind_v: float32 [8192, 16, 128], P(('sfc', 'sub')), may hold values from -6 to 6
- vert_w: float32 [8192, 16, 128], P(('sfc', 'sub')), may hold values from -6 to 6
- geopot: float32 [8192, 16, 128], P(('sfc', 'sub')), may hold values from -6 to 6
- elem_mass: float32 [8192, 16], P(('sfc', 'sub')), may hold values from 0.25 to 4
- deriv_x: float32 [16, 16], replicated, may hold values from -1.5 to 1.5
- deriv_y: float32 [16, 16], replicated, may hold values from -1.5 to 1.5
- col_inverse: float32 [128, 128], replicated, may hold values from 0 to 1, as said below
- element_cell: int32 [256, 32], P(('sfc', 'sub')), may hold values from 0 to 31, each once within a row
Outputs:
- temp_out: float32 [8192, 16, 128], P(('sfc', 'sub'))
- tracer_out: float32 [8192, 16, 128], P(('sfc', 'sub'))
- wind_u_out: float32 [8192, 16, 128], P(('sfc', 'sub'))
- wind_v_out: float32 [8192, 16, 128], P(('sfc', 'sub'))
- vert_w_out: float32 [8192, 16, 128], P(('sfc', 'sub'))
- geopot_out: float32 [8192, 16, 128], P(('sfc', 'sub'))
Inputs may be any that keep to these rules, and one draw needn't show every extreme that they name: `element_cell`: each device's row names every cell of its tile once. `col_inverse`: an approximate inverse of the derivative of r at a reference column state: symmetric, with positive entries.
All inputs are finite; a program needn't handle non-finite values.
Results may differ from a plain program's by a relative error of at most 0.0001.
Values sent between devices are 32-bit elements; how exact they have to be, the bound alone decides.
A program may use at most 64 MiB of HBM per device.

v0:
```python
import jax
import jax.numpy as jnp
from jax import lax
from jax.experimental import pallas as pl
from jax.experimental.pallas import tpu as pltpu
from jax.sharding import PartitionSpec as P

TX = 4
TY = 8
LEV = 128
NEWTON = 3
PITCH = 16
ROWS = 3 * TY + 1
NODES = ROWS * PITCH
STRIP = 64
FIELDS = 6

time_step = 0.4
visc_coef = 0.1
buoyancy = 0.5
gravity_step = 0.5
column_couple = 0.25

F32 = jnp.float32
BF16 = jnp.bfloat16
MESH = pl.DeviceIdType.MESH

SIDES = ((0, -1), (0, 1), (-1, 0), (1, 0), (-1, -1), (-1, 1), (1, -1), (1, 1))
OPPOSITE = (1, 0, 3, 2, 7, 6, 5, 4)
OFFSET = (0, 32, 64, 80, 96, 104, 112, 120)
COUNT = (32, 32, 16, 16, 8, 8, 8, 8)
CORNER_NODE = (0, 12, NODES - PITCH, NODES - PITCH + 12)


def iota(shape, dim):
    return lax.broadcasted_iota(jnp.int32, shape, dim)


def halves(x):
    high = x.astype(BF16)
    return high, (x - high.astype(F32)).astype(BF16)


def stack2(x):
    high, low = halves(x)
    return jnp.concatenate([high, low], axis=0)


def stack3(x):
    high, low = halves(x)
    return jnp.concatenate([high, low, high], axis=0)


def weight3(x):
    high, low = halves(x)
    return jnp.where(iota(x.shape, 1) < 2 * (x.shape[1] // 3), high.astype(F32), low.astype(F32)).astype(BF16)


def mm(a, b):
    return jnp.dot(a, b, preferred_element_type=F32)


def exact(a, b):
    return jnp.dot(a, b, preferred_element_type=F32, precision=lax.Precision.HIGHEST)


def onehot(cond):
    return jnp.where(cond, 1.0, 0.0).astype(F32)


def block_diag(matrix, cols):
    left = onehot(iota((STRIP, 16), 0) % 16 == iota((STRIP, 16), 1))
    right = onehot(iota((16, cols), 1) % 16 == iota((16, cols), 0))
    spread = exact(exact(left, matrix), right)
    same = (iota((STRIP, cols), 1) % STRIP) // 16 == iota((STRIP, cols), 0) // 16
    return jnp.where(same, spread, 0.0)


def node_point(node, point):
    return (node // PITCH == (point % 16) // 4) & (node % PITCH == 3 * (point // 16) + point % 4)


def gather_rim(grid, send):
    for k in range(grid.shape[0]):
        send[k, 0:ROWS] = grid[k, pl.ds(0, ROWS, stride=PITCH)]
        send[k, 32 : 32 + ROWS] = grid[k, pl.ds(12, ROWS, stride=PITCH)]
        send[k, 64:80] = grid[k, 0:16]
        send[k, 80:96] = grid[k, NODES - 16 : NODES]
        for corner, node in enumerate(CORNER_NODE):
            send[k, 96 + 8 * corner : 97 + 8 * corner] = grid[k, node : node + 1]


def add_rim(grid, recv):
    for k in range(grid.shape[0]):
        for first, rows in ((0, pl.ds(0, ROWS, stride=PITCH)), (32, pl.ds(12, ROWS, stride=PITCH))):
            grid[k, rows] = grid[k, rows] + recv[k, first : first + ROWS]
        grid[k, 0:16] = grid[k, 0:16] + recv[k, 64:80]
        grid[k, NODES - 16 : NODES] = grid[k, NODES - 16 : NODES] + recv[k, 80:96]
        for corner, node in enumerate(CORNER_NODE):
            grid[k, node : node + 1] = grid[k, node : node + 1] + recv[k, 96 + 8 * corner : 97 + 8 * corner]


def step_kernel(
    pot_in, tracer_in, u_in, v_in, w_in, geo_in, mass_in, dx_in, dy_in, col_in, cells, cells_row,
    out,
    xin, xc, mid, s1, s2, s3, mgrid, rinv, mcol, kmat, inv,
    send0, recv0, send1, recv1, send2, recv2, send3, recv3,
    load_sem, send_sem, recv_sem,
):
    row = lax.axis_index("sfc")
    col = lax.axis_index("sub")
    n_row = lax.axis_size("sfc")
    n_col = lax.axis_size("sub")

    def device(side):
        return (lax.rem(row + side[0] + n_row, n_row), lax.rem(col + side[1] + n_col, n_col))

    barrier = pltpu.get_barrier_semaphore()
    for side in SIDES:
        pl.semaphore_signal(barrier, inc=1, device_id=device(side), device_id_type=MESH)

    sources = (geo_in, w_in, pot_in, tracer_in, u_in, v_in)
    loads = [pltpu.make_async_copy(ref, xin.at[k], load_sem.at[k]) for k, ref in enumerate(sources)]
    for load in loads:
        load.start()

    def exchange(turn, send, recv):
        copies = []
        for k in range(8):
            copies.append(
                pltpu.make_async_remote_copy(
                    src_ref=send.at[:, pl.ds(OFFSET[k], COUNT[k])],
                    dst_ref=recv.at[:, pl.ds(OFFSET[OPPOSITE[k]], COUNT[k])],
                    send_sem=send_sem.at[turn, k],
                    recv_sem=recv_sem.at[turn, OPPOSITE[k]],
                    device_id=device(SIDES[k]),
                    device_id_type=MESH,
                )
            )
        return copies

    def invert(c, carry):
        slot = jnp.int32(0)
        for j in range(TX * TY):
            slot = jnp.where(cells[0, j] == c, j, slot)
        inv[c] = slot
        return carry

    lax.fori_loop(0, TX * TY, invert, 0)

    dx = dx_in[...]
    dy = dy_in[...]
    lap = exact(dx, dx) + exact(dy, dy)
    lap_blk = block_diag(lap, 3 * STRIP)
    deriv3 = weight3(jnp.concatenate([block_diag(dx, 3 * STRIP), block_diag(dy, 3 * STRIP)], axis=0))
    spread3 = onehot(node_point(iota((STRIP, 3 * STRIP), 1) % STRIP, iota((STRIP, 3 * STRIP), 0)))
    lap_nodes = exact(block_diag(lap, STRIP), spread3)
    gather2 = onehot(node_point(iota((STRIP, 2 * STRIP), 0), iota((STRIP, 2 * STRIP), 1) % STRIP)).astype(BF16)
    spread2 = onehot(node_point(iota((STRIP, 2 * STRIP), 1) % STRIP, iota((STRIP, 2 * STRIP), 0))).astype(BF16)

    for send in (send0, send1, send2, send3):
        send[...] = jnp.zeros_like(send)
    for grid in (s1, s2, s3, mgrid):
        grid[:, 0:16] = jnp.zeros((grid.shape[0], 16, LEV), F32)

    def accumulate(grid, start, vals):
        head = pl.ds(start, 16)
        tail = pl.ds(pl.multiple_of(start + 16, 16), STRIP - 16)
        for k in range(grid.shape[0]):
            part = vals[:, k * LEV : (k + 1) * LEV]
            grid[k, head] = grid[k, head] + part[0:16]
            grid[k, tail] = part[16:]

    def scaled_strip(grid, here, inverse, count):
        return jnp.concatenate([grid[k, here] * inverse for k in range(count)], axis=1)

    def mass_strip(ey, carry):
        points = []
        for ex in range(TX):
            chosen = jnp.where(cells_row[...] == TX * ey + ex, mass_in[...], 0.0)
            points.append(jnp.broadcast_to(jnp.sum(chosen, axis=1, keepdims=True), (16, LEV)))
        strip_mass = jnp.concatenate(points, axis=0)
        mcol[pl.ds(pl.multiple_of(STRIP * ey, STRIP), STRIP)] = strip_mass
        accumulate(mgrid, pl.multiple_of(48 * ey, 16), mm(gather2, stack2(strip_mass)))
        wide = jnp.concatenate([strip_mass, strip_mass[:, :STRIP]], axis=1)
        kmat[0, ey] = weight3(mm(gather2, stack2(wide * lap_blk)))
        kmat[1, ey] = weight3(mm(gather2, stack2(wide * lap_nodes)))
        return carry

    lax.fori_loop(0, TY, mass_strip, 0)
    gather_rim(mgrid, send0)
    pl.semaphore_wait(barrier, 8)
    mass_copies = exchange(0, send0, recv0)
    for copy in mass_copies:
        copy.start()

    for load in loads:
        load.wait()

    def strip_of(ref, ey, fields):
        return jnp.concatenate([ref[k, pl.ds(TX * ey, TX)].reshape(STRIP, LEV) for k in fields], axis=1)

    def tend_strip(ey, carry):
        points = pl.ds(pl.multiple_of(STRIP * ey, STRIP), STRIP)
        for ex in range(TX):
            slot = inv[TX * ey + ex]
            for k in range(FIELDS):
                xc[k, TX * ey + ex] = xin[k, slot]
        x = strip_of(xc, ey, range(FIELDS))
        x3 = stack3(x)
        slopes = mm(deriv3, x3[:, : 4 * LEV])
        sx = slopes[:STRIP]
        sy = slopes[STRIP:]
        pot = x[:, 2 * LEV : 3 * LEV]
        u = x[:, 4 * LEV : 5 * LEV]
        v = x[:, 5 * LEV : 6 * LEV]

        def advect(k):
            cols = slice(k * LEV, (k + 1) * LEV)
            return -(u * sx[:, cols] + v * sy[:, cols])

        tend = [advect(2), advect(3), -sx[:, :LEV], -sy[:, :LEV], advect(1) + buoyancy * pot]
        weight = mcol[points]
        weighted = jnp.concatenate([t * weight for t in tend], axis=1)
        start = pl.multiple_of(48 * ey, 16)
        accumulate(s1, start, mm(gather2, stack2(weighted)))
        accumulate(s2, start, mm(kmat[0, ey], x3[:, 2 * LEV :]))
        return carry

    lax.fori_loop(0, TY, tend_strip, 0)
    gather_rim(s1, send1)
    tend_copies = exchange(1, send1, recv1)
    for copy in tend_copies:
        copy.start()

    for copy in mass_copies:
        copy.wait()
    add_rim(mgrid, recv0)
    total_mass = mgrid[0]
    rinv[...] = jnp.where(total_mass > 0.0, 1.0 / jnp.where(total_mass > 0.0, total_mass, 1.0), 0.0)

    for copy in tend_copies:
        copy.wait()
    add_rim(s1, recv1)

    def lap_strip(source, scale):
        def body(ey, carry):
            start = pl.multiple_of(48 * ey, 16)
            here = pl.ds(start, STRIP)
            inverse = rinv[here] * scale
            nodal = scaled_strip(source, here, inverse, 4)
            vals = mm(kmat[1, ey], stack3(nodal))
            if source is s1:
                for k in range(4):
                    s2[k, here] = s2[k, here] + vals[:, k * LEV : (k + 1) * LEV]
            else:
                accumulate(s3, start, vals)
            return carry

        return body

    lax.fori_loop(0, TY, lap_strip(s1, time_step), 0)
    gather_rim(s2, send2)
    first_copies = exchange(2, send2, recv2)
    for copy in first_copies:
        copy.start()

    def mid_strip(ey, carry):
        here = pl.ds(pl.multiple_of(48 * ey, 16), STRIP)
        inverse = rinv[here] * time_step
        nodal = scaled_strip(s1, here, inverse, 5)
        change = mm(spread2, stack2(nodal))
        state = strip_of(xc, ey, (2, 3, 4, 5, 1)) + change
        for k in range(5):
            mid[k, pl.ds(TX * ey, TX)] = state[:, k * LEV : (k + 1) * LEV].reshape(TX, 16, LEV)
        return carry

    lax.fori_loop(0, TY, mid_strip, 0)

    for copy in first_copies:
        copy.wait()
    add_rim(s2, recv2)
    lax.fori_loop(0, TY, lap_strip(s2, 1.0), 0)
    gather_rim(s3, send3)
    second_copies = exchange(3, send3, recv3)
    for copy in second_copies:
        copy.start()

    col_high, col_low = halves(col_in[...])
    col3 = jnp.concatenate([col_high, col_high, col_low], axis=0)
    lane = iota((128, LEV), 1)

    def newton_rows(part, carry):
        elems = pl.ds(8 * part, 8)
        geo = xc[0, elems].reshape(128, LEV)
        target = geo + gravity_step * mid[4, elems].reshape(128, LEV)
        phi = target
        for _ in range(NEWTON):
            above = jnp.where(lane == LEV - 1, 0.0, pltpu.roll(phi, LEV - 1, 1))
            flux = jnp.tanh(above - phi)
            below = jnp.where(lane == 0, 0.0, pltpu.roll(flux, 1, 1))
            resid = phi - target - column_couple * (flux - below)
            high, low = halves(resid)
            phi = phi - mm(jnp.concatenate([high, low, high], axis=1), col3)
        mid[4, elems] = phi.reshape(8, 16, LEV)
        return carry

    lax.fori_loop(0, 4, newton_rows, 0)

    def place_column(j, carry):
        phi = mid[4, cells[0, j]]
        out[5, j] = phi
        out[4, j] = (phi - xc[0, cells[0, j]]) / gravity_step
        return carry

    lax.fori_loop(0, TX * TY, place_column, 0)

    for copy in second_copies:
        copy.wait()
    add_rim(s3, recv3)

    def final_strip(ey, carry):
        here = pl.ds(pl.multiple_of(48 * ey, 16), STRIP)
        inverse = rinv[here] * visc_coef
        nodal = scaled_strip(s3, here, inverse, 4)
        final = strip_of(mid, ey, range(4)) - mm(spread2, stack2(nodal))
        for k in range(4):
            mid[k, pl.ds(TX * ey, TX)] = final[:, k * LEV : (k + 1) * LEV].reshape(TX, 16, LEV)
        return carry

    lax.fori_loop(0, TY, final_strip, 0)

    def place_fields(j, carry):
        for k in range(4):
            out[k, j] = mid[k, cells[0, j]]
        return carry

    lax.fori_loop(0, TX * TY, place_fields, 0)


def store_kernel(fields, *refs):
    outs, sem = refs[:FIELDS], refs[FIELDS]
    copies = [pltpu.make_async_copy(fields.at[k], outs[k], sem.at[k]) for k in range(FIELDS)]
    for copy in copies:
        copy.start()
    for copy in copies:
        copy.wait()


def per_device(pot_temp, tracer, wind_u, wind_v, vert_w, geopot, elem_mass, deriv_x, deriv_y, col_inverse, element_cell):
    shape = pot_temp.shape
    vmem = pl.BlockSpec(memory_space=pltpu.VMEM)
    smem = pl.BlockSpec(memory_space=pltpu.SMEM)
    hbm = pl.BlockSpec(memory_space=pl.ANY)
    rim = sum(COUNT)
    fields = pl.pallas_call(
        step_kernel,
        out_shape=pltpu.VMEM((FIELDS,) + shape, F32),
        in_specs=[hbm] * 6 + [vmem] * 4 + [smem, vmem],
        out_specs=vmem,
        scratch_shapes=[
            pltpu.VMEM((FIELDS,) + shape, F32),
            pltpu.VMEM((FIELDS,) + shape, F32),
            pltpu.VMEM((5,) + shape, F32),
            pltpu.VMEM((5, NODES, LEV), F32),
            pltpu.VMEM((4, NODES, LEV), F32),
            pltpu.VMEM((4, NODES, LEV), F32),
            pltpu.VMEM((1, NODES, LEV), F32),
            pltpu.VMEM((NODES, LEV), F32),
            pltpu.VMEM((512, LEV), F32),
            pltpu.VMEM((2, TY, STRIP, 3 * STRIP), BF16),
            pltpu.SMEM((TX * TY,), jnp.int32),
            pltpu.VMEM((1, rim, LEV), F32),
            pltpu.VMEM((1, rim, LEV), F32),
            pltpu.VMEM((5, rim, LEV), F32),
            pltpu.VMEM((5, rim, LEV), F32),
            pltpu.VMEM((4, rim, LEV), F32),
            pltpu.VMEM((4, rim, LEV), F32),
            pltpu.VMEM((4, rim, LEV), F32),
            pltpu.VMEM((4, rim, LEV), F32),
            pltpu.SemaphoreType.DMA((6,)),
            pltpu.SemaphoreType.DMA((4, 8)),
            pltpu.SemaphoreType.DMA((4, 8)),
        ],
        compiler_params=pltpu.CompilerParams(collective_id=0, has_side_effects=True, vmem_limit_bytes=62 << 20),
    )(pot_temp, tracer, wind_u, wind_v, vert_w, geopot, elem_mass.T, deriv_x, deriv_y, col_inverse, element_cell, element_cell)
    result = jax.ShapeDtypeStruct(shape, F32)
    return tuple(
        pl.pallas_call(
            store_kernel,
            out_shape=[result] * FIELDS,
            in_specs=[vmem],
            out_specs=[hbm] * FIELDS,
            scratch_shapes=[pltpu.SemaphoreType.DMA((FIELDS,))],
            compiler_params=pltpu.CompilerParams(vmem_limit_bytes=48 << 20),
        )(fields)
    )


def solution(mesh):
    field = P(("sfc", "sub"), None, None)
    flat = P(("sfc", "sub"), None)
    return jax.shard_map(
        per_device,
        mesh=mesh,
        in_specs=(field,) * 6 + (flat, P(), P(), P(), flat),
        out_specs=(field,) * 6,
        check_vma=False,
    )
```

profile of v0, /device:TPU:1, one launch (start us, length us, event | category | flops | bytes accessed | tf_op | source)
XLA Modules:
  0.0 38.5 jit_solution(2988441613181623415)
XLA Ops:
  0.6 36.7 %shard_map.154.fields = f32[6,32,16,128]{3,2,1,0:T(8,128)S(1)} custom-call(f32[32,16,128]{2,1,0:T(8,128)} %pot_in.1, f32[32,16,128]{2,1,0:T(8,128)} %tracer_in.1, f32[32,16,128]{2,1,0:T(8,128)} %u_in.1, f32[32,16,128]{2,1,0:T(8,128)} %v_in.1, f32[32,16,128]{2,1,0:T(8,128)} %w_in.1, f32[32,16,128]{2,1,0:T(8,128)} %geo_in.1, f32[16,32]{1,0:T(8,128)} %bitcast.1, ...), custom_call_target="tpu_custom_call" | custom-call | tf_op jit(solution)/shard_map/pallas_call | solution.py:356
  37.3 1.2 %shard_map.155 = (f32[32,16,128]{2,1,0:T(8,128)}, f32[32,16,128]{2,1,0:T(8,128)}, f32[32,16,128]{2,1,0:T(8,128)}, f32[32,16,128]{2,1,0:T(8,128)}, f32[32,16,128]{2,1,0:T(8,128)}, /*index=5*/f32[32,16,128]{2,1,0:T(8,128)}) custom-call(f32[6,32,16,128]{3,2,1,0:T(8,128)S(1)} %shard_map.154.fields), custom_call_target="tpu_custom_call" | custom-call | tf_op jit(solution)/shard_map/pallas_call | solution.py:389
where the time goes:
time: 38.6 us; the launch traced here: 38.5 us
  Pallas kernels  37.9 us (98%)
  between operations  0.64 us (2%)
    pallas_call x1, Pallas kernels, per_device(): pl.pallas_call(step_kernel, out_shape=pltpu.VMEM((FIELDS,) + shape, F32),...  36.7 us
    pallas_call x1, Pallas kernels, per_device(): pl.pallas_call(store_kernel, out_shape=[result] * FIELDS, in_specs=[vmem]...  1.19 us

commit v1 on v0

--- a/solution.py
+++ b/solution.py
@@ -187,7 +187,7 @@
         kmat[1, ey] = weight3(mm(gather2, stack2(wide * lap_nodes)))
         return carry
 
-    lax.fori_loop(0, TY, mass_strip, 0)
+    lax.fori_loop(0, TY, mass_strip, 0, unroll=True)
     gather_rim(mgrid, send0)
     pl.semaphore_wait(barrier, 8)
     mass_copies = exchange(0, send0, recv0)
@@ -227,7 +227,7 @@
         accumulate(s2, start, mm(kmat[0, ey], x3[:, 2 * LEV :]))
         return carry
 
-    lax.fori_loop(0, TY, tend_strip, 0)
+    lax.fori_loop(0, TY, tend_strip, 0, unroll=True)
     gather_rim(s1, send1)
     tend_copies = exchange(1, send1, recv1)
     for copy in tend_copies:
@@ -259,7 +259,7 @@
 
         return body
 
-    lax.fori_loop(0, TY, lap_strip(s1, time_step), 0)
+    lax.fori_loop(0, TY, lap_strip(s1, time_step), 0, unroll=True)
     gather_rim(s2, send2)
     first_copies = exchange(2, send2, recv2)
     for copy in first_copies:
@@ -275,12 +275,12 @@
             mid[k, pl.ds(TX * ey, TX)] = state[:, k * LEV : (k + 1) * LEV].reshape(TX, 16, LEV)
         return carry
 
-    lax.fori_loop(0, TY, mid_strip, 0)
+    lax.fori_loop(0, TY, mid_strip, 0, unroll=True)
 
     for copy in first_copies:
         copy.wait()
     add_rim(s2, recv2)
-    lax.fori_loop(0, TY, lap_strip(s2, 1.0), 0)
+    lax.fori_loop(0, TY, lap_strip(s2, 1.0), 0, unroll=True)
     gather_rim(s3, send3)
     second_copies = exchange(3, send3, recv3)
     for copy in second_copies:
@@ -305,7 +305,7 @@
         mid[4, elems] = phi.reshape(8, 16, LEV)
         return carry
 
-    lax.fori_loop(0, 4, newton_rows, 0)
+    lax.fori_loop(0, 4, newton_rows, 0, unroll=True)
 
     def place_column(j, carry):
         phi = mid[4, cells[0, j]]
@@ -313,7 +313,7 @@
         out[4, j] = (phi - xc[0, cells[0, j]]) / gravity_step
         return carry
 
-    lax.fori_loop(0, TX * TY, place_column, 0)
+    lax.fori_loop(0, TX * TY, place_column, 0, unroll=True)
 
     for copy in second_copies:
         copy.wait()
@@ -328,14 +328,14 @@
             mid[k, pl.ds(TX * ey, TX)] = final[:, k * LEV : (k + 1) * LEV].reshape(TX, 16, LEV)
         return carry
 
-    lax.fori_loop(0, TY, final_strip, 0)
+    lax.fori_loop(0, TY, final_strip, 0, unroll=True)
 
     def place_fields(j, carry):
         for k in range(4):
             out[k, j] = mid[k, cells[0, j]]
         return carry
 
-    lax.fori_loop(0, TX * TY, place_fields, 0)
+    lax.fori_loop(0, TX * TY, place_fields, 0, unroll=True)
 
 
 def store_kernel(fields, *refs):

time: 38.6 us -> 32.6 us (0.84)
  Pallas kernels: 37.9 us -> 31.9 us
    pallas_call x1, Pallas kernels: 36.7 us -> 30.7 us  [per_device(): pl.pallas_call(step_kernel, out_shape=pltpu.VMEM((FIELDS,) + shape, F32),...]
where the time goes in v1:
time: 32.6 us; the launch traced here: 32.5 us
  Pallas kernels  31.9 us (98%)
  between operations  0.64 us (2%)
    pallas_call x1, Pallas kernels, per_device(): pl.pallas_call(step_kernel, out_shape=pltpu.VMEM((FIELDS,) + shape, F32),...  30.7 us
    pallas_call x1, Pallas kernels, per_device(): pl.pallas_call(store_kernel, out_shape=[result] * FIELDS, in_specs=[vmem]...  1.19 us

profile of v1, /device:TPU:1, one launch (start us, length us, event | category | flops | bytes accessed | tf_op | source)
XLA Modules:
  0.0 32.5 jit_solution(7219201349324420627)
XLA Ops:
  0.6 30.7 %shard_map.154.fields = f32[6,32,16,128]{3,2,1,0:T(8,128)S(1)} custom-call(f32[32,16,128]{2,1,0:T(8,128)} %pot_in.1, f32[32,16,128]{2,1,0:T(8,128)} %tracer_in.1, f32[32,16,128]{2,1,0:T(8,128)} %u_in.1, f32[32,16,128]{2,1,0:T(8,128)} %v_in.1, f32[32,16,128]{2,1,0:T(8,128)} %w_in.1, f32[32,16,128]{2,1,0:T(8,128)} %geo_in.1, f32[16,32]{1,0:T(8,128)} %bitcast.1, ...), custom_call_target="tpu_custom_call" | custom-call | tf_op jit(solution)/shard_map/pallas_call | solution.py:356
  31.3 1.2 %shard_map.155 = (f32[32,16,128]{2,1,0:T(8,128)}, f32[32,16,128]{2,1,0:T(8,128)}, f32[32,16,128]{2,1,0:T(8,128)}, f32[32,16,128]{2,1,0:T(8,128)}, f32[32,16,128]{2,1,0:T(8,128)}, /*index=5*/f32[32,16,128]{2,1,0:T(8,128)}) custom-call(f32[6,32,16,128]{3,2,1,0:T(8,128)S(1)} %shard_map.154.fields), custom_call_target="tpu_custom_call" | custom-call | tf_op jit(solution)/shard_map/pallas_call | solution.py:389

commit v2 on v1

v2 whole, which is shorter than its diff:
```python
import jax
import jax.numpy as jnp
import numpy as np
from jax import lax
from jax.experimental import pallas as pl
from jax.experimental.pallas import tpu as pltpu
from jax.sharding import PartitionSpec as P

TX = 4
TY = 8
LEV = 128
NEWTON = 3
PITCH = 16
ROWS = 3 * TY + 1
NODES = ROWS * PITCH
STRIP = 64
FIELDS = 6

time_step = 0.4
visc_coef = 0.1
buoyancy = 0.5
gravity_step = 0.5
column_couple = 0.25

F32 = jnp.float32
BF16 = jnp.bfloat16
MESH = pl.DeviceIdType.MESH

SIDES = ((0, -1), (0, 1), (-1, 0), (1, 0), (-1, -1), (-1, 1), (1, -1), (1, 1))
OPPOSITE = (1, 0, 3, 2, 7, 6, 5, 4)
OFFSET = (0, 32, 64, 88, 112, 120, 128, 136)
COUNT = (32, 32, 24, 24, 8, 8, 8, 8)
RIM = 144
LINE_COUNT = (25, 25, 13, 13, 1, 1, 1, 1)
LINES = (
    (0, 25, 0, 16), (32, 25, 12, 16), (64, 13, 0, 1), (88, 13, 384, 1),
    (112, 1, 0, 1), (120, 1, 12, 1), (128, 1, 384, 1), (136, 1, 396, 1),
)
ARMS = (
    (25, 3, 1, 1), (28, 3, 385, 1), (57, 3, 9, 1), (60, 3, 393, 1),
    (77, 3, 16, 16), (80, 3, 28, 16), (101, 3, 336, 16), (104, 3, 348, 16),
    (113, 3, 1, 1), (116, 3, 16, 16), (121, 3, 9, 1), (124, 3, 28, 16),
    (129, 3, 385, 1), (132, 3, 336, 16), (137, 3, 393, 1), (140, 3, 348, 16),
)


def rim_tables():
    node = np.full(RIM, -1)
    line = np.zeros(RIM)
    for group in (LINES, ARMS):
        for first, rows, start, stride in group:
            node[first : first + rows] = start + stride * np.arange(rows)
            line[first : first + rows] = group is LINES
    place = np.arange(RIM) - 4000.0
    slot = np.zeros(RIM)
    lane_node = np.full(RIM, -1)
    for k in range(8):
        mine = np.arange(OFFSET[k], OFFSET[k] + COUNT[k])
        theirs = mine - OFFSET[k] + OFFSET[OPPOSITE[k]]
        slot[mine] = k
        lane_node[mine] = node[theirs]
        known = node[theirs] >= 0
        ny = node[theirs] // PITCH + 3 * TY * SIDES[k][0]
        nx = node[theirs] % PITCH + 3 * TX * SIDES[k][1]
        place[mine[known]] = ((ny + 8) * 64 + nx + 8)[known]
    unique = line.copy()
    unique[112:] = 0
    unique[[64, 76, 88, 100]] = 0
    rows = np.stack([np.broadcast_to(t[:, None], (RIM, LEV)) for t in (place, line, unique, slot)])
    lanes = np.full((3, 8, 2 * LEV), -9000.0)
    lanes[:, :, :RIM] = np.stack([lane_node, place, slot])[:, None]
    return rows.astype(np.float32), lanes.astype(np.float32)


def iota(shape, dim):
    return lax.broadcasted_iota(jnp.int32, shape, dim)


def halves(x):
    high = x.astype(BF16)
    return high, (x - high.astype(F32)).astype(BF16)


def stack2(x):
    high, low = halves(x)
    return jnp.concatenate([high, low], axis=0)


def stack3(x):
    high, low = halves(x)
    return jnp.concatenate([high, low, high], axis=0)


def weight3(x):
    high, low = halves(x)
    return jnp.where(iota(x.shape, 1) < 2 * (x.shape[1] // 3), high.astype(F32), low.astype(F32)).astype(BF16)


def mm(a, b):
    return jnp.dot(a, b, preferred_element_type=F32)


def exact(a, b):
    return jnp.dot(a, b, preferred_element_type=F32, precision=lax.Precision.HIGHEST)


def onehot(cond):
    return jnp.where(cond, 1.0, 0.0).astype(F32)


def block_diag(matrix, cols):
    left = onehot(iota((STRIP, 16), 0) % 16 == iota((STRIP, 16), 1))
    right = onehot(iota((16, cols), 1) % 16 == iota((16, cols), 0))
    spread = exact(exact(left, matrix), right)
    same = (iota((STRIP, cols), 1) % STRIP) // 16 == iota((STRIP, cols), 0) // 16
    return jnp.where(same, spread, 0.0)


def node_point(node, point):
    return (node // PITCH == (point % 16) // 4) & (node % PITCH == 3 * (point // 16) + point % 4)


def gather_rim(grid, send, groups, blocks, first=0):
    for n, k in enumerate(blocks):
        for group in groups:
            for row, rows, start, stride in group:
                send[first + n, row : row + rows] = grid[k, pl.ds(start, rows, stride=stride)]


def add_rim(grid, recv, blocks):
    for k in blocks:
        for row, rows, start, stride in LINES:
            nodes = pl.ds(start, rows, stride=stride)
            grid[k, nodes] = grid[k, nodes] + recv[k, row : row + rows]


def lanes_of(ref, blocks):
    return jnp.concatenate([ref[k] for k in blocks], axis=1)


def swap_sides(x):
    return jnp.concatenate([x[OFFSET[k] : OFFSET[k] + COUNT[k]] for k in OPPOSITE], axis=0)


def mm3(weight, x):
    w_high, w_low = halves(weight[:, :RIM])
    high, low = halves(x)
    return mm(w_high, high) + mm(w_high, low) + mm(w_low, high)


def step_kernel(
    pot_in, tracer_in, u_in, v_in, w_in, geo_in, mass_hbm, dx_hbm, dy_hbm, col_hbm, cells_hbm, row_hbm, lane_hbm,
    out,
    mass_in, dx_in, dy_in, col_in, cells, cells_row, row_tab, lane_tab,
    xin, xc, mid, s1, s2, s3, s4, mgrid, rinv, mcol, kmat, inv,
    send0, recv0, send1, recv1, send2, recv2, send3, recv3, local, foreign, rim_inv,
    load_sem, send_sem, recv_sem,
):
    row = lax.axis_index("sfc")
    col = lax.axis_index("sub")
    n_row = lax.axis_size("sfc")
    n_col = lax.axis_size("sub")

    def device(side):
        return (lax.rem(row + side[0] + n_row, n_row), lax.rem(col + side[1] + n_col, n_col))

    barrier = pltpu.get_barrier_semaphore()
    for side in SIDES:
        pl.semaphore_signal(barrier, inc=1, device_id=device(side), device_id_type=MESH)

    sources = (geo_in, w_in, pot_in, tracer_in, u_in, v_in)
    loads = [pltpu.make_async_copy(ref, xin.at[k], load_sem.at[k]) for k, ref in enumerate(sources)]
    smalls = [
        pltpu.make_async_copy(source, place, load_sem.at[FIELDS + k])
        for k, (source, place) in enumerate(
            (
                (cells_hbm, cells), (cells_hbm, cells_row), (mass_hbm, mass_in), (dx_hbm, dx_in), (dy_hbm, dy_in),
                (col_hbm, col_in), (row_hbm, row_tab), (lane_hbm, lane_tab),
            )
        )
    ]
    for load in smalls + loads:
        load.start()

    def exchange(turn, send, recv, counts, offset=OFFSET):
        copies = []
        for k in (2, 3, 4, 5, 6, 7, 0, 1):
            copies.append(
                pltpu.make_async_remote_copy(
                    src_ref=send.at[:, pl.ds(offset[k], counts[k])],
                    dst_ref=recv.at[:, pl.ds(offset[OPPOSITE[k]], counts[k])],
                    send_sem=send_sem.at[turn, k],
                    recv_sem=recv_sem.at[turn, OPPOSITE[k]],
                    device_id=device(SIDES[k]),
                    device_id_type=MESH,
                )
            )
        return copies

    for load in smalls:
        load.wait()

    def invert(c, carry):
        slot = jnp.int32(0)
        for j in range(TX * TY):
            slot = jnp.where(cells[0, j] == c, j, slot)
        inv[c] = slot
        return carry

    lax.fori_loop(0, TX * TY, invert, 0)

    dx = dx_in[...]
    dy = dy_in[...]
    deriv3 = weight3(jnp.concatenate([block_diag(dx, 3 * STRIP), block_diag(dy, 3 * STRIP)], axis=0))
    gather2 = onehot(node_point(iota((STRIP, 2 * STRIP), 0), iota((STRIP, 2 * STRIP), 1) % STRIP)).astype(BF16)
    spread2 = onehot(node_point(iota((STRIP, 2 * STRIP), 1) % STRIP, iota((STRIP, 2 * STRIP), 0))).astype(BF16)

    for send in (send0, send1, local):
        send[...] = jnp.zeros_like(send)
    for grid in (s1, s2, s3, s4, mgrid):
        grid[:, 0:16] = jnp.zeros((grid.shape[0], 16, LEV), F32)

    def accumulate(grid, start, vals):
        head = pl.ds(start, 16)
        tail = pl.ds(pl.multiple_of(start + 16, 16), STRIP - 16)
        for k in range(grid.shape[0]):
            part = vals[:, k * LEV : (k + 1) * LEV]
            grid[k, head] = grid[k, head] + part[0:16]
            grid[k, tail] = part[16:]

    def scaled_strip(grid, here, inverse, count):
        return jnp.concatenate([grid[k, here] * inverse for k in range(count)], axis=1)

    def mass_strip(ey, carry):
        points = []
        for ex in range(TX):
            chosen = jnp.where(cells_row[...] == TX * ey + ex, mass_in[...], 0.0)
            points.append(jnp.broadcast_to(jnp.sum(chosen, axis=1, keepdims=True), (16, LEV)))
        strip_mass = jnp.concatenate(points, axis=0)
        mcol[pl.ds(pl.multiple_of(STRIP * ey, STRIP), STRIP)] = strip_mass
        accumulate(mgrid, pl.multiple_of(48 * ey, 16), mm(gather2, stack2(strip_mass)))
        return carry

    lax.fori_loop(0, TY, mass_strip, 0, unroll=True)
    gather_rim(mgrid, send0, (LINES, ARMS), range(1))
    for load in loads:
        load.wait()

    def strip_of(ref, ey, fields):
        return jnp.concatenate([ref[k, pl.ds(TX * ey, TX)].reshape(STRIP, LEV) for k in fields], axis=1)

    def tend_strip(ey, carry):
        points = pl.ds(pl.multiple_of(STRIP * ey, STRIP), STRIP)
        for ex in range(TX):
            slot = inv[TX * ey + ex]
            for k in range(FIELDS):
                xc[k, TX * ey + ex] = xin[k, slot]
        x = strip_of(xc, ey, range(FIELDS))
        slopes = mm(deriv3, stack3(x[:, : 4 * LEV]))
        sx = slopes[:STRIP]
        sy = slopes[STRIP:]
        pot = x[:, 2 * LEV : 3 * LEV]
        u = x[:, 4 * LEV : 5 * LEV]
        v = x[:, 5 * LEV : 6 * LEV]

        def advect(k):
            cols = slice(k * LEV, (k + 1) * LEV)
            return -(u * sx[:, cols] + v * sy[:, cols])

        tend = [advect(2), advect(3), -sx[:, :LEV], -sy[:, :LEV], advect(1) + buoyancy * pot]
        weight = mcol[points]
        weighted = jnp.concatenate([t * weight for t in tend], axis=1)
        start = pl.multiple_of(48 * ey, 16)
        accumulate(s1, start, mm(gather2, stack2(weighted)))
        return carry

    lax.fori_loop(0, TY, tend_strip, 0, unroll=True)
    gather_rim(s1, send1, (LINES,), range(5))
    pl.semaphore_wait(barrier, 8)
    mass_copies = exchange(0, send0, recv0, COUNT)
    tend_copies = exchange(1, send1.at[pl.ds(0, 4)], recv1.at[pl.ds(0, 4)], LINE_COUNT)
    for copy in mass_copies + tend_copies:
        copy.start()

    lap = exact(dx, dx) + exact(dy, dy)
    lap_blk = block_diag(lap, 3 * STRIP)
    spread3 = onehot(node_point(iota((STRIP, 3 * STRIP), 1) % STRIP, iota((STRIP, 3 * STRIP), 0)))
    lap_nodes = exact(block_diag(lap, STRIP), spread3)

    def matrix_strip(ey, carry):
        strip_mass = mcol[pl.ds(pl.multiple_of(STRIP * ey, STRIP), STRIP)]
        wide = jnp.concatenate([strip_mass, strip_mass[:, :STRIP]], axis=1)
        kmat[0, ey] = weight3(mm(gather2, stack2(wide * lap_blk)))
        kmat[1, ey] = weight3(mm(gather2, stack2(wide * lap_nodes)))
        return carry

    lax.fori_loop(0, TY, matrix_strip, 0, unroll=True)

    same_place = onehot(row_tab[0][:, :1] == lane_tab[1][0:1, :RIM]).astype(BF16)

    def merge(x):
        high, low = halves(x)
        return mm(same_place, high) + mm(same_place, low)

    def reciprocal(total):
        return jnp.where(total > 0.0, 1.0 / jnp.where(total > 0.0, total, 1.0), 0.0)

    line = row_tab[1]
    unique = row_tab[2]
    node_row = iota((NODES, LEV), 0) // PITCH
    node_col = iota((NODES, LEV), 0) % PITCH
    inside = (node_row > 0) & (node_row < ROWS - 1) & (node_col > 0) & (node_col < 12)
    rinv[1] = jnp.where(inside, reciprocal(mgrid[0]), 0.0)

    def first_strip(ey, carry):
        start = pl.multiple_of(48 * ey, 16)
        here = pl.ds(start, STRIP)
        rims = onehot((iota((STRIP, 2 * LEV), 0) + start).astype(F32) == lane_tab[0][0:1])
        nodal = jnp.concatenate([scaled_strip(s1, here, rinv[1, here] * time_step, 4), rims], axis=1)
        response = mm(kmat[1, ey], stack3(nodal))
        own = mm(kmat[0, ey], stack3(strip_of(xc, ey, (2, 3, 4, 5))))
        accumulate(s2, start, jnp.concatenate([response[:, : 4 * LEV] + own, response[:, 4 * LEV :]], axis=1))
        return carry

    lax.fori_loop(0, TY, first_strip, 0, unroll=True)
    gather_rim(s2, local, (LINES, ARMS), range(6))
    send2[...] = local[4:6]
    matrix_copies = exchange(2, send2, recv2, LINE_COUNT)
    vert_copies = exchange(4, send1.at[pl.ds(4, 1)], recv1.at[pl.ds(4, 1)], LINE_COUNT)
    for copy in matrix_copies + vert_copies:
        copy.start()

    def second_strip(ey, carry):
        start = pl.multiple_of(48 * ey, 16)
        here = pl.ds(start, STRIP)
        accumulate(s3, start, mm(kmat[1, ey], stack3(scaled_strip(s2, here, rinv[1, here], 6))))
        return carry

    lax.fori_loop(0, TY, second_strip, 0, unroll=True)
    gather_rim(s3, local, (LINES,), range(6), 6)

    for copy in mass_copies:
        copy.wait()
    rim_inv[...] = reciprocal(merge(recv0[0]) + line * send0[0])
    for copy in tend_copies:
        copy.wait()
    outer = jnp.concatenate(
        [
            (jnp.where(line > 0.0, recv1[k], 0.0) + unique * send1[k]) * (rim_inv[...] * time_step)
            for k in range(4)
        ],
        axis=1,
    )
    outer = swap_sides(outer)
    one = lanes_of(local, range(4)) + mm3(lanes_of(local, range(4, 6)), outer)
    two = lanes_of(local, range(6, 10)) + mm3(lanes_of(local, range(10, 12)), outer)
    for k in range(4):
        for side in range(8):
            mine = slice(OFFSET[side], OFFSET[side] + COUNT[side])
            first = 2 * OFFSET[side]
            send3[k, first : first + COUNT[side]] = one[mine, k * LEV : (k + 1) * LEV]
            send3[k, first + COUNT[side] : first + 2 * COUNT[side]] = two[mine, k * LEV : (k + 1) * LEV]
    visc_copies = exchange(
        3, send3, recv3, [m + n for m, n in zip(COUNT, LINE_COUNT)], [2 * first for first in OFFSET]
    )
    for copy in visc_copies:
        copy.start()

    for k in range(4):
        foreign[k] = one[:, k * LEV : (k + 1) * LEV]
    add_rim(mgrid, recv0, range(1))
    rinv[0] = reciprocal(mgrid[0])
    add_rim(s1, recv1, range(4))
    rim_nodes = lanes_of(s2, range(4, 6))
    own = lanes_of(s2, range(4)) + mm3(rim_nodes, outer)
    for k in range(4):
        s2[k] = own[:, k * LEV : (k + 1) * LEV]

    def third_strip(ey, carry):
        start = pl.multiple_of(48 * ey, 16)
        here = pl.ds(start, STRIP)
        accumulate(s4, start, mm(kmat[1, ey], stack3(scaled_strip(s2, here, rinv[0, here], 4))))
        return carry

    lax.fori_loop(0, TY, third_strip, 0, unroll=True)

    for copy in vert_copies:
        copy.wait()
    add_rim(s1, recv1, range(4, 5))

    def mid_strip(ey, carry):
        here = pl.ds(pl.multiple_of(48 * ey, 16), STRIP)
        nodal = scaled_strip(s1, here, rinv[0, here] * time_step, 5)
        change = mm(spread2, stack2(nodal))
        state = strip_of(xc, ey, (2, 3, 4, 5, 1)) + change
        for k in range(5):
            mid[k, pl.ds(TX * ey, TX)] = state[:, k * LEV : (k + 1) * LEV].reshape(TX, 16, LEV)
        return carry

    lax.fori_loop(0, TY, mid_strip, 0, unroll=True)

    col_high, col_low = halves(col_in[...])
    col3 = jnp.concatenate([col_high, col_high, col_low], axis=0)
    lane = iota((128, LEV), 1)

    def newton_rows(part, carry):
        elems = pl.ds(8 * part, 8)
        geo = xc[0, elems].reshape(128, LEV)
        target = geo + gravity_step * mid[4, elems].reshape(128, LEV)
        phi = target
        for _ in range(NEWTON):
            above = jnp.where(lane == LEV - 1, 0.0, pltpu.roll(phi, LEV - 1, 1))
            flux = jnp.tanh(above - phi)
            below = jnp.where(lane == 0, 0.0, pltpu.roll(flux, 1, 1))
            resid = phi - target - column_couple * (flux - below)
            high, low = halves(resid)
            phi = phi - mm(jnp.concatenate([high, low, high], axis=1), col3)
        mid[4, elems] = phi.reshape(8, 16, LEV)
        return carry

    lax.fori_loop(0, 4, newton_rows, 0, unroll=True)

    def place_column(j, carry):
        phi = mid[4, cells[0, j]]
        out[5, j] = phi
        out[4, j] = (phi - xc[0, cells[0, j]]) / gravity_step
        return carry

    lax.fori_loop(0, TX * TY, place_column, 0, unroll=True)

    for copy in matrix_copies:
        copy.wait()
    own_block = (row_tab[3][:, :1] == lane_tab[2][0:1]) & (line[:, :1] > 0.0)
    rim_matrix = jnp.where(own_block, lanes_of(recv2, range(2)), 0.0)
    inverse = rim_inv[...]
    own_rim = jnp.concatenate([foreign[k] * (line * inverse) for k in range(4)], axis=1)

    def received(part):
        def rows(k, side):
            first = 2 * OFFSET[side] + part * COUNT[side]
            return recv3[k, first : first + COUNT[side]]

        return [jnp.concatenate([rows(k, side) for side in range(8)], axis=0) for k in range(4)]

    for copy in visc_copies:
        copy.wait()
    arrived = merge(jnp.concatenate(received(0), axis=1)) * jnp.concatenate([inverse] * 4, axis=1)
    turned = jnp.concatenate([jnp.where(line > 0.0, rows, 0.0) for rows in received(1)], axis=1)
    outside = mm3(rim_matrix, arrived + own_rim) + turned
    inner = mm3(rim_nodes, swap_sides(arrived * jnp.concatenate([unique] * 4, axis=1)))
    for k in range(4):
        foreign[k] = outside[:, k * LEV : (k + 1) * LEV]
        s4[k] = s4[k] + inner[:, k * LEV : (k + 1) * LEV]
    add_rim(s4, foreign, range(4))

    def final_strip(ey, carry):
        here = pl.ds(pl.multiple_of(48 * ey, 16), STRIP)
        nodal = scaled_strip(s4, here, rinv[0, here] * visc_coef, 4)
        final = strip_of(mid, ey, range(4)) - mm(spread2, stack2(nodal))
        for k in range(4):
            mid[k, pl.ds(TX * ey, TX)] = final[:, k * LEV : (k + 1) * LEV].reshape(TX, 16, LEV)
        return carry

    lax.fori_loop(0, TY, final_strip, 0, unroll=True)

    def place_fields(j, carry):
        for k in range(4):
            out[k, j] = mid[k, cells[0, j]]
        return carry

    lax.fori_loop(0, TX * TY, place_fields, 0, unroll=True)


def store_kernel(fields, *refs):
    outs, sem = refs[:FIELDS], refs[FIELDS]
    copies = [pltpu.make_async_copy(fields.at[k], outs[k], sem.at[k]) for k in range(FIELDS)]
    for copy in copies:
        copy.start()
    for copy in copies:
        copy.wait()


def per_device(pot_temp, tracer, wind_u, wind_v, vert_w, geopot, elem_mass, deriv_x, deriv_y, col_inverse, element_cell):
    shape = pot_temp.shape
    vmem = pl.BlockSpec(memory_space=pltpu.VMEM)
    hbm = pl.BlockSpec(memory_space=pl.ANY)
    rows, lanes = rim_tables()
    fields = pl.pallas_call(
        step_kernel,
        out_shape=pltpu.VMEM((FIELDS,) + shape, F32),
        in_specs=[hbm] * 13,
        out_specs=vmem,
        scratch_shapes=[
            pltpu.VMEM((16, TX * TY), F32),
            pltpu.VMEM((16, 16), F32),
            pltpu.VMEM((16, 16), F32),
            pltpu.VMEM((LEV, LEV), F32),
            pltpu.SMEM((1, TX * TY), jnp.int32),
            pltpu.VMEM((1, TX * TY), jnp.int32),
            pltpu.VMEM(rows.shape, F32),
            pltpu.VMEM(lanes.shape, F32),
            pltpu.VMEM((FIELDS,) + shape, F32),
            pltpu.VMEM((FIELDS,) + shape, F32),
            pltpu.VMEM((5,) + shape, F32),
            pltpu.VMEM((5, NODES, LEV), F32),
            pltpu.VMEM((6, NODES, LEV), F32),
            pltpu.VMEM((6, NODES, LEV), F32),
            pltpu.VMEM((4, NODES, LEV), F32),
            pltpu.VMEM((1, NODES, LEV), F32),
            pltpu.VMEM((2, NODES, LEV), F32),
            pltpu.VMEM((512, LEV), F32),
            pltpu.VMEM((2, TY, STRIP, 3 * STRIP), BF16),
            pltpu.SMEM((TX * TY,), jnp.int32),
        ]
        + [pltpu.VMEM((blocks, RIM, LEV), F32) for blocks in (1, 1, 5, 5, 2, 2)]
        + [pltpu.VMEM((4, 2 * RIM, LEV), F32)] * 2
        + [pltpu.VMEM((blocks, RIM, LEV), F32) for blocks in (12, 4)]
        + [
            pltpu.VMEM((RIM, LEV), F32),
            pltpu.SemaphoreType.DMA((FIELDS + 8,)),
            pltpu.SemaphoreType.DMA((5, 8)),
            pltpu.SemaphoreType.DMA((5, 8)),
        ],
        compiler_params=pltpu.CompilerParams(collective_id=0, has_side_effects=True, vmem_limit_bytes=62 << 20),
    )(pot_temp, tracer, wind_u, wind_v, vert_w, geopot, elem_mass.T, deriv_x, deriv_y, col_inverse, element_cell, rows, lanes)
    result = jax.ShapeDtypeStruct(shape, F32)
    return tuple(
        pl.pallas_call(
            store_kernel,
            out_shape=[result] * FIELDS,
            in_specs=[vmem],
            out_specs=[hbm] * FIELDS,
            scratch_shapes=[pltpu.SemaphoreType.DMA((FIELDS,))],
            compiler_params=pltpu.CompilerParams(vmem_limit_bytes=48 << 20),
        )(fields)
    )


def solution(mesh):
    field = P(("sfc", "sub"), None, None)
    flat = P(("sfc", "sub"), None)
    return jax.shard_map(
        per_device,
        mesh=mesh,
        in_specs=(field,) * 6 + (flat, P(), P(), P(), flat),
        out_specs=(field,) * 6,
        check_vma=False,
    )
```

time: 32.6 us -> 27.1 us (0.83)
  Pallas kernels: 31.9 us -> 26.3 us
    pallas_call x1, Pallas kernels: 30.7 us -> 25.1 us  [per_device(): pl.pallas_call(step_kernel, out_shape=pltpu.VMEM((FIELDS,) + shape, F32),...]
where the time goes in v2:
time: 27.1 us; the launch traced here: 27 us
  Pallas kernels  26.3 us (97%)
  between operations  0.64 us (2%)
    pallas_call x1, Pallas kernels, per_device(): pl.pallas_call(step_kernel, out_shape=pltpu.VMEM((FIELDS,) + shape, F32),...  25.1 us
    pallas_call x1, Pallas kernels, per_device(): pl.pallas_call(store_kernel, out_shape=[result] * FIELDS, in_specs=[vmem]...  1.19 us

profile of v2, /device:TPU:1, one launch (start us, length us, event | category | flops | bytes accessed | tf_op | source)
XLA Modules:
  0.0 27.0 jit_solution(16870001962941024167)
XLA Ops:
  0.6 25.1 %shard_map.172.fields = f32[6,32,16,128]{3,2,1,0:T(8,128)S(1)} custom-call(f32[32,16,128]{2,1,0:T(8,128)} %pot_in.1, f32[32,16,128]{2,1,0:T(8,128)} %tracer_in.1, f32[32,16,128]{2,1,0:T(8,128)} %u_in.1, f32[32,16,128]{2,1,0:T(8,128)} %v_in.1, f32[32,16,128]{2,1,0:T(8,128)} %w_in.1, f32[32,16,128]{2,1,0:T(8,128)} %geo_in.1, f32[16,32]{1,0:T(8,128)} %bitcast.1, ...), custom_call_target="tpu_custom_call" | custom-call | tf_op jit(solution)/shard_map/pallas_call | solution.py:488
  25.8 1.2 %shard_map.173 = (f32[32,16,128]{2,1,0:T(8,128)}, f32[32,16,128]{2,1,0:T(8,128)}, f32[32,16,128]{2,1,0:T(8,128)}, f32[32,16,128]{2,1,0:T(8,128)}, f32[32,16,128]{2,1,0:T(8,128)}, /*index=5*/f32[32,16,128]{2,1,0:T(8,128)}) custom-call(f32[6,32,16,128]{3,2,1,0:T(8,128)S(1)} %shard_map.172.fields), custom_call_target="tpu_custom_call" | custom-call | tf_op jit(solution)/shard_map/pallas_call | solution.py:528

commit v3 on v2

--- a/solution.py
+++ b/solution.py
@@ -28,29 +28,47 @@
 
 SIDES = ((0, -1), (0, 1), (-1, 0), (1, 0), (-1, -1), (-1, 1), (1, -1), (1, 1))
 OPPOSITE = (1, 0, 3, 2, 7, 6, 5, 4)
-OFFSET = (0, 32, 64, 88, 112, 120, 128, 136)
-COUNT = (32, 32, 24, 24, 8, 8, 8, 8)
-RIM = 144
+OFFSET = (0, 40, 80, 112, 144, 160, 176, 192)
+COUNT = (40, 40, 32, 32, 16, 16, 16, 16)
+RIM = 208
 LINE_COUNT = (25, 25, 13, 13, 1, 1, 1, 1)
+NEAR_COUNT = (31, 31, 19, 19, 7, 7, 7, 7)
+FULL_COUNT = (37, 37, 25, 25, 13, 13, 13, 13)
+DIRECT = (2, 3, 0, 1)
+DIAGONAL = (4, 5, 6, 7)
+TURN_ROWS = (32, 32, 24, 24)
+TURN_OFFSET = (0, 32, 64, 88)
+TURN_RIM = 112
 LINES = (
-    (0, 25, 0, 16), (32, 25, 12, 16), (64, 13, 0, 1), (88, 13, 384, 1),
-    (112, 1, 0, 1), (120, 1, 12, 1), (128, 1, 384, 1), (136, 1, 396, 1),
+    (0, 25, 0, 16), (40, 25, 12, 16), (80, 13, 0, 1), (112, 13, 384, 1),
+    (144, 1, 0, 1), (160, 1, 12, 1), (176, 1, 384, 1), (192, 1, 396, 1),
 )
-ARMS = (
-    (25, 3, 1, 1), (28, 3, 385, 1), (57, 3, 9, 1), (60, 3, 393, 1),
-    (77, 3, 16, 16), (80, 3, 28, 16), (101, 3, 336, 16), (104, 3, 348, 16),
-    (113, 3, 1, 1), (116, 3, 16, 16), (121, 3, 9, 1), (124, 3, 28, 16),
-    (129, 3, 385, 1), (132, 3, 336, 16), (137, 3, 393, 1), (140, 3, 348, 16),
+NEAR = (
+    (25, 3, 1, 1), (28, 3, 385, 1), (65, 3, 9, 1), (68, 3, 393, 1),
+    (93, 3, 16, 16), (96, 3, 28, 16), (125, 3, 336, 16), (128, 3, 348, 16),
+    (145, 3, 1, 1), (148, 3, 16, 16), (161, 3, 9, 1), (164, 3, 28, 16),
+    (177, 3, 385, 1), (180, 3, 336, 16), (193, 3, 393, 1), (196, 3, 348, 16),
 )
+FAR = (
+    (31, 3, 4, 1), (34, 3, 388, 1), (71, 3, 6, 1), (74, 3, 390, 1),
+    (99, 3, 64, 16), (102, 3, 76, 16), (131, 3, 288, 16), (134, 3, 300, 16),
+    (151, 3, 4, 1), (154, 3, 64, 16), (167, 3, 6, 1), (170, 3, 76, 16),
+    (183, 3, 388, 1), (186, 3, 288, 16), (199, 3, 390, 1), (202, 3, 300, 16),
+)
+SIDE_LINES = ((0, 25, 0, 16), (32, 25, 12, 16), (64, 13, 0, 1), (88, 13, 384, 1))
+CORNER_LINES = LINES[4:]
+PLACE, KNOWN, LINE, UNIQUE, EDGE, LATE, CLOSE, SLOT = range(8)
 
 
 def rim_tables():
     node = np.full(RIM, -1)
     line = np.zeros(RIM)
-    for group in (LINES, ARMS):
+    close = np.zeros(RIM)
+    for group in (LINES, NEAR, FAR):
         for first, rows, start, stride in group:
             node[first : first + rows] = start + stride * np.arange(rows)
             line[first : first + rows] = group is LINES
+            close[first : first + rows] = group is not FAR
     place = np.arange(RIM) - 4000.0
     slot = np.zeros(RIM)
     lane_node = np.full(RIM, -1)
@@ -63,10 +81,14 @@
         ny = node[theirs] // PITCH + 3 * TY * SIDES[k][0]
         nx = node[theirs] % PITCH + 3 * TX * SIDES[k][1]
         place[mine[known]] = ((ny + 8) * 64 + nx + 8)[known]
-    unique = line.copy()
-    unique[112:] = 0
-    unique[[64, 76, 88, 100]] = 0
-    rows = np.stack([np.broadcast_to(t[:, None], (RIM, LEV)) for t in (place, line, unique, slot)])
+    corner = np.zeros(RIM)
+    corner[[0, 24, 40, 64, 80, 92, 112, 124]] = 1
+    unique = line * (slot < 4) * np.where(slot < 2, 1, 1 - corner)
+    edge = line * (slot < 4) * (1 - corner)
+    late = np.where(slot < 4, corner, node >= 0)
+    rows = np.zeros((RIM, LEV))
+    for column, table in enumerate((place, node >= 0, line, unique, edge, late, close, slot)):
+        rows[:, column] = table
     lanes = np.full((3, 8, 2 * LEV), -9000.0)
     lanes[:, :, :RIM] = np.stack([lane_node, place, slot])[:, None]
     return rows.astype(np.float32), lanes.astype(np.float32)
@@ -127,15 +149,24 @@
                 send[first + n, row : row + rows] = grid[k, pl.ds(start, rows, stride=stride)]
 
 
-def add_rim(grid, recv, blocks):
+def add_rim(grid, recv, blocks, lines=LINES):
     for k in blocks:
-        for row, rows, start, stride in LINES:
+        for row, rows, start, stride in lines:
             nodes = pl.ds(start, rows, stride=stride)
             grid[k, nodes] = grid[k, nodes] + recv[k, row : row + rows]
 
 
 def lanes_of(ref, blocks):
     return jnp.concatenate([ref[k] for k in blocks], axis=1)
+
+
+def spread_rows(parts):
+    filled = []
+    for k, part in enumerate(parts):
+        filled.append(part)
+        if part.shape[0] < COUNT[k]:
+            filled.append(jnp.zeros((COUNT[k] - part.shape[0], part.shape[1]), F32))
+    return jnp.concatenate(filled, axis=0)
 
 
 def swap_sides(x):
@@ -153,7 +184,7 @@
     out,
     mass_in, dx_in, dy_in, col_in, cells, cells_row, row_tab, lane_tab,
     xin, xc, mid, s1, s2, s3, s4, mgrid, rinv, mcol, kmat, inv,
-    send0, recv0, send1, recv1, send2, recv2, send3, recv3, local, foreign, rim_inv,
+    send1, recv0, recv1, send2, recv2, local, away, foreign, rim_inv,
     load_sem, send_sem, recv_sem,
 ):
     row = lax.axis_index("sfc")
@@ -182,19 +213,23 @@
     for load in smalls + loads:
         load.start()
 
-    def exchange(turn, send, recv, counts, offset=OFFSET):
+    def exchange(turn, send, recv, sides, start, counts, blocks=None, land=None):
         copies = []
-        for k in (2, 3, 4, 5, 6, 7, 0, 1):
+        for k in sides:
+            source, target = start[k], (land or start)[OPPOSITE[k]]
+            lanes = pl.ds(0, send.shape[0]) if blocks is None else pl.ds(*blocks)
             copies.append(
                 pltpu.make_async_remote_copy(
-                    src_ref=send.at[:, pl.ds(offset[k], counts[k])],
-                    dst_ref=recv.at[:, pl.ds(offset[OPPOSITE[k]], counts[k])],
+                    src_ref=send.at[lanes, pl.ds(source, counts[k])],
+                    dst_ref=recv.at[lanes, pl.ds(target, counts[k])],
                     send_sem=send_sem.at[turn, k],
                     recv_sem=recv_sem.at[turn, OPPOSITE[k]],
                     device_id=device(SIDES[k]),
                     device_id_type=MESH,
                 )
             )
+        for copy in copies:
+            copy.start()
         return copies
 
     for load in smalls:
@@ -215,7 +250,7 @@
     gather2 = onehot(node_point(iota((STRIP, 2 * STRIP), 0), iota((STRIP, 2 * STRIP), 1) % STRIP)).astype(BF16)
     spread2 = onehot(node_point(iota((STRIP, 2 * STRIP), 1) % STRIP, iota((STRIP, 2 * STRIP), 0))).astype(BF16)
 
-    for send in (send0, send1, local):
+    for send in (send1, local):
         send[...] = jnp.zeros_like(send)
     for grid in (s1, s2, s3, s4, mgrid):
         grid[:, 0:16] = jnp.zeros((grid.shape[0], 16, LEV), F32)
@@ -242,7 +277,7 @@
         return carry
 
     lax.fori_loop(0, TY, mass_strip, 0, unroll=True)
-    gather_rim(mgrid, send0, (LINES, ARMS), range(1))
+    gather_rim(mgrid, send1, (LINES, NEAR, FAR), range(1), 4)
     for load in loads:
         load.wait()
 
@@ -275,12 +310,42 @@
         return carry
 
     lax.fori_loop(0, TY, tend_strip, 0, unroll=True)
-    gather_rim(s1, send1, (LINES,), range(5))
+    gather_rim(s1, send1, (LINES, NEAR, FAR), range(4))
+    gather_rim(s1, send1, (LINES,), range(4, 5), 5)
     pl.semaphore_wait(barrier, 8)
-    mass_copies = exchange(0, send0, recv0, COUNT)
-    tend_copies = exchange(1, send1.at[pl.ds(0, 4)], recv1.at[pl.ds(0, 4)], LINE_COUNT)
-    for copy in mass_copies + tend_copies:
-        copy.start()
+    far_start = [first + n for first, n in zip(OFFSET, LINE_COUNT)]
+    far_count = [n - m for m, n in zip(LINE_COUNT, FULL_COUNT)]
+    line_copies = exchange(0, send1, recv0, DIRECT, OFFSET, LINE_COUNT, (0, 5), TURN_OFFSET)
+    late_copies = exchange(1, send1, recv1, DIAGONAL, OFFSET, FULL_COUNT, (0, 5))
+    late_copies += exchange(2, send1, recv1, DIRECT, far_start, far_count, (0, 5))
+
+    col_high, col_low = halves(col_in[...])
+    col3 = jnp.concatenate(
+        [jnp.concatenate([col_high, col_low], axis=1), jnp.concatenate([col_high, jnp.zeros_like(col_low)], axis=1)],
+        axis=0,
+    )
+
+    def newton(elements, which):
+        change = {}
+        for ey in sorted({ey for ey, _ in elements}):
+            here = pl.ds(48 * ey, STRIP)
+            change[ey] = mm(spread2, stack2(s1[4, here] * (rinv[which, here] * time_step)))
+        for first in range(0, len(elements), 8):
+            part = elements[first : first + 8]
+            rows = [change[ey][16 * ex : 16 * ex + 16] + xc[1, TX * ey + ex] for ey, ex in part]
+            geo = jnp.concatenate([xc[0, TX * ey + ex] for ey, ex in part], axis=0)
+            target = geo + gravity_step * jnp.concatenate(rows, axis=0)
+            phi = target
+            lane = iota(phi.shape, 1)
+            for _ in range(NEWTON):
+                above = jnp.where(lane == LEV - 1, 0.0, pltpu.roll(phi, LEV - 1, 1))
+                flux = jnp.tanh(above - phi)
+                below = jnp.where(lane == 0, 0.0, pltpu.roll(flux, 1, 1))
+                resid = phi - target - column_couple * (flux - below)
+                step = mm(jnp.concatenate(halves(resid), axis=1), col3)
+                phi = phi - (step[:, :LEV] + step[:, LEV:])
+            for n, (ey, ex) in enumerate(part):
+                mid[TX * ey + ex] = phi[16 * n : 16 * n + 16]
 
     lap = exact(dx, dx) + exact(dy, dy)
     lap_blk = block_diag(lap, 3 * STRIP)
@@ -296,7 +361,10 @@
 
     lax.fori_loop(0, TY, matrix_strip, 0, unroll=True)
 
-    same_place = onehot(row_tab[0][:, :1] == lane_tab[1][0:1, :RIM]).astype(BF16)
+    def column(kind):
+        return row_tab[:, kind : kind + 1]
+
+    same_place = onehot(column(PLACE) == lane_tab[1][0:1, :RIM]).astype(BF16)
 
     def merge(x):
         high, low = halves(x)
@@ -305,8 +373,6 @@
     def reciprocal(total):
         return jnp.where(total > 0.0, 1.0 / jnp.where(total > 0.0, total, 1.0), 0.0)
 
-    line = row_tab[1]
-    unique = row_tab[2]
     node_row = iota((NODES, LEV), 0) // PITCH
     node_col = iota((NODES, LEV), 0) % PITCH
     inside = (node_row > 0) & (node_row < ROWS - 1) & (node_col > 0) & (node_col < 12)
@@ -323,12 +389,11 @@
         return carry
 
     lax.fori_loop(0, TY, first_strip, 0, unroll=True)
-    gather_rim(s2, local, (LINES, ARMS), range(6))
-    send2[...] = local[4:6]
-    matrix_copies = exchange(2, send2, recv2, LINE_COUNT)
-    vert_copies = exchange(4, send1.at[pl.ds(4, 1)], recv1.at[pl.ds(4, 1)], LINE_COUNT)
-    for copy in matrix_copies + vert_copies:
-        copy.start()
+    gather_rim(s2, local, (LINES, NEAR), range(6))
+    late_copies += exchange(3, local, away, DIRECT, OFFSET, NEAR_COUNT, (4, 2))
+    late_copies += exchange(3, local, away, DIAGONAL, OFFSET, NEAR_COUNT, (0, 6))
+    vert_copies = exchange(4, send1, recv1, DIRECT, OFFSET, LINE_COUNT, (5, 1))
+    late_copies += exchange(4, send1, recv1, DIAGONAL, OFFSET, LINE_COUNT, (5, 1))
 
     def second_strip(ey, carry):
         start = pl.multiple_of(48 * ey, 16)
@@ -338,116 +403,111 @@
 
     lax.fori_loop(0, TY, second_strip, 0, unroll=True)
     gather_rim(s3, local, (LINES,), range(6), 6)
-
-    for copy in mass_copies:
+    late_copies += exchange(5, local, away, DIRECT, OFFSET, LINE_COUNT, (10, 2))
+    late_copies += exchange(5, local, away, DIAGONAL, OFFSET, LINE_COUNT, (6, 6))
+
+    newton([(ey, ex) for ey in range(1, TY - 1) for ex in (1, 2)], 1)
+
+    def wide(x):
+        return jnp.concatenate([x] * 4, axis=1)
+
+    for copy in line_copies:
         copy.wait()
-    rim_inv[...] = reciprocal(merge(recv0[0]) + line * send0[0])
-    for copy in tend_copies:
-        copy.wait()
-    outer = jnp.concatenate(
-        [
-            (jnp.where(line > 0.0, recv1[k], 0.0) + unique * send1[k]) * (rim_inv[...] * time_step)
-            for k in range(4)
-        ],
-        axis=1,
+    edge = column(EDGE) > 0.0
+    side_lines = spread_rows(
+        [lanes_of(recv0, range(5))[first : first + rows] for first, rows in zip(TURN_OFFSET, TURN_ROWS)]
+        + [jnp.zeros((16, 5 * LEV), F32)] * 4
     )
-    outer = swap_sides(outer)
-    one = lanes_of(local, range(4)) + mm3(lanes_of(local, range(4, 6)), outer)
-    two = lanes_of(local, range(6, 10)) + mm3(lanes_of(local, range(10, 12)), outer)
-    for k in range(4):
-        for side in range(8):
-            mine = slice(OFFSET[side], OFFSET[side] + COUNT[side])
-            first = 2 * OFFSET[side]
-            send3[k, first : first + COUNT[side]] = one[mine, k * LEV : (k + 1) * LEV]
-            send3[k, first + COUNT[side] : first + 2 * COUNT[side]] = two[mine, k * LEV : (k + 1) * LEV]
-    visc_copies = exchange(
-        3, send3, recv3, [m + n for m, n in zip(COUNT, LINE_COUNT)], [2 * first for first in OFFSET]
-    )
-    for copy in visc_copies:
-        copy.start()
-
-    for k in range(4):
-        foreign[k] = one[:, k * LEV : (k + 1) * LEV]
-    add_rim(mgrid, recv0, range(1))
+    edge_mass = jnp.where(edge, side_lines[:, 4 * LEV :] + send1[4], 1.0)
+    edge_vals = jnp.where(edge, side_lines[:, : 4 * LEV] + lanes_of(send1, range(4)), 0.0)
+    outer = swap_sides(edge_vals * wide(time_step / edge_mass))
+
+    def send_turn(turn, vals):
+        for k in range(4):
+            for side in DIRECT:
+                rows, start, first = TURN_ROWS[side], OFFSET[side], TURN_OFFSET[side]
+                send2[turn, k, first : first + rows] = vals[start : start + rows, k * LEV : (k + 1) * LEV]
+        counts = (NEAR_COUNT, LINE_COUNT)[turn]
+        return exchange(6 + turn, send2.at[turn], recv2.at[turn], DIRECT, TURN_OFFSET, counts)
+
+    turn_copies = send_turn(0, lanes_of(local, range(4)) + mm3(lanes_of(local, range(4, 6)), outer))
+    turn_copies += send_turn(1, lanes_of(local, range(6, 10)) + mm3(lanes_of(local, range(10, 12)), outer))
+
+    add_rim(mgrid, recv0.at[pl.ds(4, 1)], range(1), SIDE_LINES)
     rinv[0] = reciprocal(mgrid[0])
-    add_rim(s1, recv1, range(4))
-    rim_nodes = lanes_of(s2, range(4, 6))
-    own = lanes_of(s2, range(4)) + mm3(rim_nodes, outer)
-    for k in range(4):
-        s2[k] = own[:, k * LEV : (k + 1) * LEV]
-
-    def third_strip(ey, carry):
-        start = pl.multiple_of(48 * ey, 16)
-        here = pl.ds(start, STRIP)
-        accumulate(s4, start, mm(kmat[1, ey], stack3(scaled_strip(s2, here, rinv[0, here], 4))))
-        return carry
-
-    lax.fori_loop(0, TY, third_strip, 0, unroll=True)
-
     for copy in vert_copies:
         copy.wait()
-    add_rim(s1, recv1, range(4, 5))
-
-    def mid_strip(ey, carry):
-        here = pl.ds(pl.multiple_of(48 * ey, 16), STRIP)
-        nodal = scaled_strip(s1, here, rinv[0, here] * time_step, 5)
-        change = mm(spread2, stack2(nodal))
-        state = strip_of(xc, ey, (2, 3, 4, 5, 1)) + change
-        for k in range(5):
-            mid[k, pl.ds(TX * ey, TX)] = state[:, k * LEV : (k + 1) * LEV].reshape(TX, 16, LEV)
-        return carry
-
-    lax.fori_loop(0, TY, mid_strip, 0, unroll=True)
-
-    col_high, col_low = halves(col_in[...])
-    col3 = jnp.concatenate([col_high, col_high, col_low], axis=0)
-    lane = iota((128, LEV), 1)
-
-    def newton_rows(part, carry):
-        elems = pl.ds(8 * part, 8)
-        geo = xc[0, elems].reshape(128, LEV)
-        target = geo + gravity_step * mid[4, elems].reshape(128, LEV)
-        phi = target
-        for _ in range(NEWTON):
-            above = jnp.where(lane == LEV - 1, 0.0, pltpu.roll(phi, LEV - 1, 1))
-            flux = jnp.tanh(above - phi)
-            below = jnp.where(lane == 0, 0.0, pltpu.roll(flux, 1, 1))
-            resid = phi - target - column_couple * (flux - below)
-            high, low = halves(resid)
-            phi = phi - mm(jnp.concatenate([high, low, high], axis=1), col3)
-        mid[4, elems] = phi.reshape(8, 16, LEV)
-        return carry
-
-    lax.fori_loop(0, 4, newton_rows, 0, unroll=True)
+    for row, rows, start, stride in LINES[:4]:
+        nodes = pl.ds(start, rows, stride=stride)
+        s1[4, nodes] = s1[4, nodes] + recv1[5, row : row + rows]
+    newton([(ey, ex) for ey in range(1, TY - 1) for ex in (0, 3)] + [(ey, ex) for ey in (0, TY - 1) for ex in (1, 2)], 0)
+
+    for copy in late_copies:
+        copy.wait()
+    known = column(KNOWN) > 0.0
+    line = column(LINE)
+    unique = column(UNIQUE)
+    side_line = (line > 0.0) & (column(SLOT) < 3.5)
+    arrived_all = jnp.where(side_line, side_lines, jnp.where(known, lanes_of(recv1, range(5)), 0.0))
+    arrived_all = arrived_all + unique * lanes_of(send1, range(5))
+    totals = merge(arrived_all)
+    rim_inv[...] = reciprocal(totals[:, 4 * LEV :])
+    rim_state = totals[:, : 4 * LEV] * wide(rim_inv[...] * time_step)
+    outer = swap_sides(unique * rim_state)
+    own_block = column(SLOT) == lane_tab[2][0:1]
+    rim_matrix = jnp.where(own_block & (column(CLOSE) > 0.0), lanes_of(away, range(4, 6)), 0.0)
+    rim_matrix2 = jnp.where(own_block & (line > 0.0), lanes_of(away, range(10, 12)), 0.0)
+    late = column(LATE) * rim_state
+    diagonal = column(SLOT) > 3.5
+    late_one = mm3(rim_matrix, late) + jnp.where(diagonal & (column(CLOSE) > 0.0), lanes_of(away, range(4)), 0.0)
+    late_two = mm3(rim_matrix2, late) + jnp.where(diagonal & (line > 0.0), lanes_of(away, range(6, 10)), 0.0)
+    add_rim(mgrid, recv1.at[pl.ds(4, 1)], range(1), CORNER_LINES)
+    rinv[0] = reciprocal(mgrid[0])
+    add_rim(s1, recv0, range(4), SIDE_LINES)
+    add_rim(s1, recv1, range(4), CORNER_LINES)
+    for row, rows, start, stride in CORNER_LINES:
+        nodes = pl.ds(start, rows, stride=stride)
+        s1[4, nodes] = s1[4, nodes] + recv1[5, row : row + rows]
+    newton([(ey, ex) for ey in (0, TY - 1) for ex in (0, 3)], 0)
+
+    rim_nodes = lanes_of(s2, range(4, 6))
+    own_sum = lanes_of(local, range(4)) + mm3(lanes_of(local, range(4, 6)), outer)
+    own_rim = jnp.where(line > 0.0, own_sum, 0.0) * wide(rim_inv[...])
+    again = lanes_of(s3, range(4)) + mm3(lanes_of(s3, range(4, 6)), outer)
+    for k in range(4):
+        s4[k] = again[:, k * LEV : (k + 1) * LEV]
 
     def place_column(j, carry):
-        phi = mid[4, cells[0, j]]
+        phi = mid[cells[0, j]]
         out[5, j] = phi
         out[4, j] = (phi - xc[0, cells[0, j]]) / gravity_step
         return carry
 
     lax.fori_loop(0, TX * TY, place_column, 0, unroll=True)
 
-    for copy in matrix_copies:
+    inverse = rim_inv[...]
+
+    def received(part, counts):
+        def rows(k, side):
+            first = TURN_OFFSET[side]
+            return recv2[part, k, first : first + counts[side]]
+
+        return jnp.concatenate(
+            [
+                spread_rows([rows(k, side) for side in range(4)] + [jnp.zeros((16, LEV), F32)] * 4)
+                for k in range(4)
+            ],
+            axis=1,
+        )
+
+    for copy in turn_copies:
         copy.wait()
-    own_block = (row_tab[3][:, :1] == lane_tab[2][0:1]) & (line[:, :1] > 0.0)
-    rim_matrix = jnp.where(own_block, lanes_of(recv2, range(2)), 0.0)
-    inverse = rim_inv[...]
-    own_rim = jnp.concatenate([foreign[k] * (line * inverse) for k in range(4)], axis=1)
-
-    def received(part):
-        def rows(k, side):
-            first = 2 * OFFSET[side] + part * COUNT[side]
-            return recv3[k, first : first + COUNT[side]]
-
-        return [jnp.concatenate([rows(k, side) for side in range(8)], axis=0) for k in range(4)]
-
-    for copy in visc_copies:
-        copy.wait()
-    arrived = merge(jnp.concatenate(received(0), axis=1)) * jnp.concatenate([inverse] * 4, axis=1)
-    turned = jnp.concatenate([jnp.where(line > 0.0, rows, 0.0) for rows in received(1)], axis=1)
+    direct = ~diagonal
+    first_turn = jnp.where(direct & (column(CLOSE) > 0.0), received(0, TURN_ROWS), 0.0) + late_one
+    arrived = merge(first_turn) * wide(inverse)
+    turned = jnp.where(direct & (line > 0.0), received(1, TURN_ROWS), 0.0) + late_two
     outside = mm3(rim_matrix, arrived + own_rim) + turned
-    inner = mm3(rim_nodes, swap_sides(arrived * jnp.concatenate([unique] * 4, axis=1)))
+    inner = mm3(rim_nodes, swap_sides((arrived + own_rim) * unique))
     for k in range(4):
         foreign[k] = outside[:, k * LEV : (k + 1) * LEV]
         s4[k] = s4[k] + inner[:, k * LEV : (k + 1) * LEV]
@@ -455,17 +515,20 @@
 
     def final_strip(ey, carry):
         here = pl.ds(pl.multiple_of(48 * ey, 16), STRIP)
-        nodal = scaled_strip(s4, here, rinv[0, here] * visc_coef, 4)
-        final = strip_of(mid, ey, range(4)) - mm(spread2, stack2(nodal))
+        inverse = rinv[0, here]
+        nodal = jnp.concatenate(
+            [(time_step * s1[k, here] - visc_coef * s4[k, here]) * inverse for k in range(4)], axis=1
+        )
+        final = strip_of(xc, ey, (2, 3, 4, 5)) + mm(spread2, stack2(nodal))
         for k in range(4):
-            mid[k, pl.ds(TX * ey, TX)] = final[:, k * LEV : (k + 1) * LEV].reshape(TX, 16, LEV)
+            xc[2 + k, pl.ds(TX * ey, TX)] = final[:, k * LEV : (k + 1) * LEV].reshape(TX, 16, LEV)
         return carry
 
     lax.fori_loop(0, TY, final_strip, 0, unroll=True)
 
     def place_fields(j, carry):
         for k in range(4):
-            out[k, j] = mid[k, cells[0, j]]
+            out[k, j] = xc[2 + k, cells[0, j]]
         return carry
 
     lax.fori_loop(0, TX * TY, place_fields, 0, unroll=True)
@@ -501,7 +564,7 @@
             pltpu.VMEM(lanes.shape, F32),
             pltpu.VMEM((FIELDS,) + shape, F32),
             pltpu.VMEM((FIELDS,) + shape, F32),
-            pltpu.VMEM((5,) + shape, F32),
+            pltpu.VMEM(shape, F32),
             pltpu.VMEM((5, NODES, LEV), F32),
             pltpu.VMEM((6, NODES, LEV), F32),
             pltpu.VMEM((6, NODES, LEV), F32),
@@ -512,14 +575,14 @@
             pltpu.VMEM((2, TY, STRIP, 3 * STRIP), BF16),
             pltpu.SMEM((TX * TY,), jnp.int32),
         ]
-        + [pltpu.VMEM((blocks, RIM, LEV), F32) for blocks in (1, 1, 5, 5, 2, 2)]
-        + [pltpu.VMEM((4, 2 * RIM, LEV), F32)] * 2
-        + [pltpu.VMEM((blocks, RIM, LEV), F32) for blocks in (12, 4)]
+        + [pltpu.VMEM((6, RIM, LEV), F32), pltpu.VMEM((5, TURN_RIM, LEV), F32), pltpu.VMEM((6, RIM, LEV), F32)]
+        + [pltpu.VMEM((2, 4, TURN_RIM, LEV), F32)] * 2
+        + [pltpu.VMEM((blocks, RIM, LEV), F32) for blocks in (12, 12, 4)]
         + [
             pltpu.VMEM((RIM, LEV), F32),
             pltpu.SemaphoreType.DMA((FIELDS + 8,)),
-            pltpu.SemaphoreType.DMA((5, 8)),
-            pltpu.SemaphoreType.DMA((5, 8)),
+            pltpu.SemaphoreType.DMA((8, 8)),
+            pltpu.SemaphoreType.DMA((8, 8)),
         ],
         compiler_params=pltpu.CompilerParams(collective_id=0, has_side_effects=True, vmem_limit_bytes=62 << 20),
     )(pot_temp, tracer, wind_u, wind_v, vert_w, geopot, elem_mass.T, deriv_x, deriv_y, col_inverse, element_cell, rows, lanes)

time: 27.1 us -> 25 us (0.923)
  the two profiles are of different devices: /device:TPU:1 before, /device:TPU:0 now
where the time goes in v3:
time: 25 us; the launch traced here: 24.9 us
  Pallas kernels  24.2 us (97%)
  between operations  0.64 us (3%)
    pallas_call x1, Pallas kernels, per_device(): pl.pallas_call(step_kernel, out_shape=pltpu.VMEM((FIELDS,) + shape, F32),...  23 us
    pallas_call x1, Pallas kernels, per_device(): pl.pallas_call(store_kernel, out_shape=[result] * FIELDS, in_specs=[vmem]...  1.19 us

profile of v3, /device:TPU:0, one launch (start us, length us, event | category | flops | bytes accessed | tf_op | source)
XLA Modules:
  0.0 24.9 jit_solution(4529757456209270854)
XLA Ops:
  0.6 23.0 %shard_map.172.fields = f32[6,32,16,128]{3,2,1,0:T(8,128)S(1)} custom-call(f32[32,16,128]{2,1,0:T(8,128)} %pot_in.1, f32[32,16,128]{2,1,0:T(8,128)} %tracer_in.1, f32[32,16,128]{2,1,0:T(8,128)} %u_in.1, f32[32,16,128]{2,1,0:T(8,128)} %v_in.1, f32[32,16,128]{2,1,0:T(8,128)} %w_in.1, f32[32,16,128]{2,1,0:T(8,128)} %geo_in.1, f32[16,32]{1,0:T(8,128)} %bitcast.1, ...), custom_call_target="tpu_custom_call" | custom-call | tf_op jit(solution)/shard_map/pallas_call | solution.py:551
  23.7 1.2 %shard_map.173 = (f32[32,16,128]{2,1,0:T(8,128)}, f32[32,16,128]{2,1,0:T(8,128)}, f32[32,16,128]{2,1,0:T(8,128)}, f32[32,16,128]{2,1,0:T(8,128)}, f32[32,16,128]{2,1,0:T(8,128)}, /*index=5*/f32[32,16,128]{2,1,0:T(8,128)}) custom-call(f32[6,32,16,128]{3,2,1,0:T(8,128)S(1)} %shard_map.172.fields), custom_call_target="tpu_custom_call" | custom-call | tf_op jit(solution)/shard_map/pallas_call | solution.py:591

commit v4 on v3

--- a/solution.py
+++ b/solution.py
@@ -174,7 +174,7 @@
 
 
 def mm3(weight, x):
-    w_high, w_low = halves(weight[:, :RIM])
+    w_high, w_low = weight if isinstance(weight, tuple) else halves(weight[:, :RIM])
     high, low = halves(x)
     return mm(w_high, high) + mm(w_high, low) + mm(w_low, high)
 
@@ -184,7 +184,7 @@
     out,
     mass_in, dx_in, dy_in, col_in, cells, cells_row, row_tab, lane_tab,
     xin, xc, mid, s1, s2, s3, s4, mgrid, rinv, mcol, kmat, inv,
-    send1, recv0, recv1, send2, recv2, local, away, foreign, rim_inv,
+    send1, recv0, recv1, recv_vert, local, away, foreign, rim_inv,
     load_sem, send_sem, recv_sem,
 ):
     row = lax.axis_index("sfc")
@@ -277,7 +277,7 @@
         return carry
 
     lax.fori_loop(0, TY, mass_strip, 0, unroll=True)
-    gather_rim(mgrid, send1, (LINES, NEAR, FAR), range(1), 4)
+    gather_rim(mgrid, send1, (LINES, NEAR, FAR), range(1), 1)
     for load in loads:
         load.wait()
 
@@ -310,14 +310,15 @@
         return carry
 
     lax.fori_loop(0, TY, tend_strip, 0, unroll=True)
-    gather_rim(s1, send1, (LINES, NEAR, FAR), range(4))
-    gather_rim(s1, send1, (LINES,), range(4, 5), 5)
+    gather_rim(s1, send1, (LINES,), range(4, 5), 0)
+    gather_rim(s1, send1, (LINES, NEAR, FAR), range(4), 2)
     pl.semaphore_wait(barrier, 8)
     far_start = [first + n for first, n in zip(OFFSET, LINE_COUNT)]
     far_count = [n - m for m, n in zip(LINE_COUNT, FULL_COUNT)]
-    line_copies = exchange(0, send1, recv0, DIRECT, OFFSET, LINE_COUNT, (0, 5), TURN_OFFSET)
-    late_copies = exchange(1, send1, recv1, DIAGONAL, OFFSET, FULL_COUNT, (0, 5))
-    late_copies += exchange(2, send1, recv1, DIRECT, far_start, far_count, (0, 5))
+    vert_copies = exchange(4, send1, recv_vert, range(8), OFFSET, LINE_COUNT, (0, 2))
+    line_copies = exchange(0, send1, recv0, DIRECT, OFFSET, LINE_COUNT, (2, 4), TURN_OFFSET)
+    line_copies += exchange(1, send1, recv1, DIAGONAL, OFFSET, FULL_COUNT, (1, 5))
+    line_copies += exchange(2, send1, recv1, DIRECT, far_start, far_count, (1, 5))
 
     col_high, col_low = halves(col_in[...])
     col3 = jnp.concatenate(
@@ -330,8 +331,8 @@
         for ey in sorted({ey for ey, _ in elements}):
             here = pl.ds(48 * ey, STRIP)
             change[ey] = mm(spread2, stack2(s1[4, here] * (rinv[which, here] * time_step)))
-        for first in range(0, len(elements), 8):
-            part = elements[first : first + 8]
+        for first in range(0, len(elements), 20):
+            part = elements[first : first + 20]
             rows = [change[ey][16 * ex : 16 * ex + 16] + xc[1, TX * ey + ex] for ey, ex in part]
             geo = jnp.concatenate([xc[0, TX * ey + ex] for ey, ex in part], axis=0)
             target = geo + gravity_step * jnp.concatenate(rows, axis=0)
@@ -390,10 +391,7 @@
 
     lax.fori_loop(0, TY, first_strip, 0, unroll=True)
     gather_rim(s2, local, (LINES, NEAR), range(6))
-    late_copies += exchange(3, local, away, DIRECT, OFFSET, NEAR_COUNT, (4, 2))
-    late_copies += exchange(3, local, away, DIAGONAL, OFFSET, NEAR_COUNT, (0, 6))
-    vert_copies = exchange(4, send1, recv1, DIRECT, OFFSET, LINE_COUNT, (5, 1))
-    late_copies += exchange(4, send1, recv1, DIAGONAL, OFFSET, LINE_COUNT, (5, 1))
+    near_copies = exchange(3, local, away, range(8), OFFSET, NEAR_COUNT, (0, 6))
 
     def second_strip(ey, carry):
         start = pl.multiple_of(48 * ey, 16)
@@ -403,77 +401,56 @@
 
     lax.fori_loop(0, TY, second_strip, 0, unroll=True)
     gather_rim(s3, local, (LINES,), range(6), 6)
-    late_copies += exchange(5, local, away, DIRECT, OFFSET, LINE_COUNT, (10, 2))
-    late_copies += exchange(5, local, away, DIAGONAL, OFFSET, LINE_COUNT, (6, 6))
-
+    far_copies = exchange(5, local, away, range(8), OFFSET, LINE_COUNT, (6, 6))
+
+    own_weight = halves(lanes_of(local, range(4, 6))[:, :RIM])
+    again_weight = halves(lanes_of(s3, range(4, 6))[:, :RIM])
+    inner_weight = halves(lanes_of(s2, range(4, 6))[:, :RIM])
     newton([(ey, ex) for ey in range(1, TY - 1) for ex in (1, 2)], 1)
 
     def wide(x):
         return jnp.concatenate([x] * 4, axis=1)
 
-    for copy in line_copies:
-        copy.wait()
-    edge = column(EDGE) > 0.0
-    side_lines = spread_rows(
-        [lanes_of(recv0, range(5))[first : first + rows] for first, rows in zip(TURN_OFFSET, TURN_ROWS)]
-        + [jnp.zeros((16, 5 * LEV), F32)] * 4
-    )
-    edge_mass = jnp.where(edge, side_lines[:, 4 * LEV :] + send1[4], 1.0)
-    edge_vals = jnp.where(edge, side_lines[:, : 4 * LEV] + lanes_of(send1, range(4)), 0.0)
-    outer = swap_sides(edge_vals * wide(time_step / edge_mass))
-
-    def send_turn(turn, vals):
-        for k in range(4):
-            for side in DIRECT:
-                rows, start, first = TURN_ROWS[side], OFFSET[side], TURN_OFFSET[side]
-                send2[turn, k, first : first + rows] = vals[start : start + rows, k * LEV : (k + 1) * LEV]
-        counts = (NEAR_COUNT, LINE_COUNT)[turn]
-        return exchange(6 + turn, send2.at[turn], recv2.at[turn], DIRECT, TURN_OFFSET, counts)
-
-    turn_copies = send_turn(0, lanes_of(local, range(4)) + mm3(lanes_of(local, range(4, 6)), outer))
-    turn_copies += send_turn(1, lanes_of(local, range(6, 10)) + mm3(lanes_of(local, range(10, 12)), outer))
-
-    add_rim(mgrid, recv0.at[pl.ds(4, 1)], range(1), SIDE_LINES)
-    rinv[0] = reciprocal(mgrid[0])
-    for copy in vert_copies:
-        copy.wait()
-    for row, rows, start, stride in LINES[:4]:
-        nodes = pl.ds(start, rows, stride=stride)
-        s1[4, nodes] = s1[4, nodes] + recv1[5, row : row + rows]
-    newton([(ey, ex) for ey in range(1, TY - 1) for ex in (0, 3)] + [(ey, ex) for ey in (0, TY - 1) for ex in (1, 2)], 0)
-
-    for copy in late_copies:
-        copy.wait()
     known = column(KNOWN) > 0.0
     line = column(LINE)
     unique = column(UNIQUE)
     side_line = (line > 0.0) & (column(SLOT) < 3.5)
-    arrived_all = jnp.where(side_line, side_lines, jnp.where(known, lanes_of(recv1, range(5)), 0.0))
-    arrived_all = arrived_all + unique * lanes_of(send1, range(5))
-    totals = merge(arrived_all)
-    rim_inv[...] = reciprocal(totals[:, 4 * LEV :])
-    rim_state = totals[:, : 4 * LEV] * wide(rim_inv[...] * time_step)
+    own_block = column(SLOT) == lane_tab[2][0:1]
+    close = column(CLOSE) > 0.0
+
+    for copy in vert_copies:
+        copy.wait()
+    add_rim(mgrid, recv_vert.at[pl.ds(1, 1)], range(1))
+    rinv[0] = reciprocal(mgrid[0])
+    for row, rows, start, stride in LINES:
+        nodes = pl.ds(start, rows, stride=stride)
+        s1[4, nodes] = s1[4, nodes] + recv_vert[0, row : row + rows]
+    newton(
+        [(ey, ex) for ey in range(1, TY - 1) for ex in (0, 3)] + [(ey, ex) for ey in (0, TY - 1) for ex in range(TX)], 0
+    )
+
+    for copy in line_copies:
+        copy.wait()
+    side_lines = spread_rows(
+        [lanes_of(recv0, range(2, 6))[first : first + rows] for first, rows in zip(TURN_OFFSET, TURN_ROWS)]
+        + [jnp.zeros((16, 4 * LEV), F32)] * 4
+    )
+    arrived_all = jnp.where(side_line, side_lines, jnp.where(known, lanes_of(recv1, range(2, 6)), 0.0))
+    mass_all = jnp.where(line > 0.0, recv_vert[1], jnp.where(known, recv1[1], 0.0))
+    rim_inv[...] = reciprocal(merge(mass_all + unique * send1[1]))
+    totals = merge(arrived_all + unique * lanes_of(send1, range(2, 6)))
+    rim_state = totals * wide(rim_inv[...] * time_step)
     outer = swap_sides(unique * rim_state)
-    own_block = column(SLOT) == lane_tab[2][0:1]
-    rim_matrix = jnp.where(own_block & (column(CLOSE) > 0.0), lanes_of(away, range(4, 6)), 0.0)
-    rim_matrix2 = jnp.where(own_block & (line > 0.0), lanes_of(away, range(10, 12)), 0.0)
-    late = column(LATE) * rim_state
-    diagonal = column(SLOT) > 3.5
-    late_one = mm3(rim_matrix, late) + jnp.where(diagonal & (column(CLOSE) > 0.0), lanes_of(away, range(4)), 0.0)
-    late_two = mm3(rim_matrix2, late) + jnp.where(diagonal & (line > 0.0), lanes_of(away, range(6, 10)), 0.0)
-    add_rim(mgrid, recv1.at[pl.ds(4, 1)], range(1), CORNER_LINES)
-    rinv[0] = reciprocal(mgrid[0])
-    add_rim(s1, recv0, range(4), SIDE_LINES)
-    add_rim(s1, recv1, range(4), CORNER_LINES)
-    for row, rows, start, stride in CORNER_LINES:
-        nodes = pl.ds(start, rows, stride=stride)
-        s1[4, nodes] = s1[4, nodes] + recv1[5, row : row + rows]
-    newton([(ey, ex) for ey in (0, TY - 1) for ex in (0, 3)], 0)
-
-    rim_nodes = lanes_of(s2, range(4, 6))
-    own_sum = lanes_of(local, range(4)) + mm3(lanes_of(local, range(4, 6)), outer)
+    for k in range(4):
+        for row, rows, start, stride in SIDE_LINES:
+            nodes = pl.ds(start, rows, stride=stride)
+            s1[k, nodes] = s1[k, nodes] + recv0[2 + k, row : row + rows]
+        for row, rows, start, stride in CORNER_LINES:
+            nodes = pl.ds(start, rows, stride=stride)
+            s1[k, nodes] = s1[k, nodes] + recv1[2 + k, row : row + rows]
+    own_sum = lanes_of(local, range(4)) + mm3(own_weight, outer)
     own_rim = jnp.where(line > 0.0, own_sum, 0.0) * wide(rim_inv[...])
-    again = lanes_of(s3, range(4)) + mm3(lanes_of(s3, range(4, 6)), outer)
+    again = lanes_of(s3, range(4)) + mm3(again_weight, outer)
     for k in range(4):
         s4[k] = again[:, k * LEV : (k + 1) * LEV]
 
@@ -486,28 +463,17 @@
     lax.fori_loop(0, TX * TY, place_column, 0, unroll=True)
 
     inverse = rim_inv[...]
-
-    def received(part, counts):
-        def rows(k, side):
-            first = TURN_OFFSET[side]
-            return recv2[part, k, first : first + counts[side]]
-
-        return jnp.concatenate(
-            [
-                spread_rows([rows(k, side) for side in range(4)] + [jnp.zeros((16, LEV), F32)] * 4)
-                for k in range(4)
-            ],
-            axis=1,
-        )
-
-    for copy in turn_copies:
+    for copy in near_copies:
         copy.wait()
-    direct = ~diagonal
-    first_turn = jnp.where(direct & (column(CLOSE) > 0.0), received(0, TURN_ROWS), 0.0) + late_one
-    arrived = merge(first_turn) * wide(inverse)
-    turned = jnp.where(direct & (line > 0.0), received(1, TURN_ROWS), 0.0) + late_two
-    outside = mm3(rim_matrix, arrived + own_rim) + turned
-    inner = mm3(rim_nodes, swap_sides((arrived + own_rim) * unique))
+    rim_matrix = jnp.where(own_block & close, lanes_of(away, range(4, 6)), 0.0)
+    first_turn = jnp.where(close, lanes_of(away, range(4)), 0.0) + mm3(rim_matrix, rim_state)
+    rim_next = merge(first_turn) * wide(inverse) + own_rim
+    outside = mm3(rim_matrix, rim_next)
+    inner = mm3(inner_weight, swap_sides(rim_next * unique))
+    for copy in far_copies:
+        copy.wait()
+    rim_matrix2 = jnp.where(own_block & (line > 0.0), lanes_of(away, range(10, 12)), 0.0)
+    outside = outside + jnp.where(line > 0.0, lanes_of(away, range(6, 10)), 0.0) + mm3(rim_matrix2, rim_state)
     for k in range(4):
         foreign[k] = outside[:, k * LEV : (k + 1) * LEV]
         s4[k] = s4[k] + inner[:, k * LEV : (k + 1) * LEV]
@@ -575,14 +541,14 @@
             pltpu.VMEM((2, TY, STRIP, 3 * STRIP), BF16),
             pltpu.SMEM((TX * TY,), jnp.int32),
         ]
-        + [pltpu.VMEM((6, RIM, LEV), F32), pltpu.VMEM((5, TURN_RIM, LEV), F32), pltpu.VMEM((6, RIM, LEV), F32)]
-        + [pltpu.VMEM((2, 4, TURN_RIM, LEV), F32)] * 2
+        + [pltpu.VMEM((6, RIM, LEV), F32), pltpu.VMEM((6, TURN_RIM, LEV), F32), pltpu.VMEM((6, RIM, LEV), F32)]
+        + [pltpu.VMEM((2, RIM, LEV), F32)]
         + [pltpu.VMEM((blocks, RIM, LEV), F32) for blocks in (12, 12, 4)]
         + [
             pltpu.VMEM((RIM, LEV), F32),
             pltpu.SemaphoreType.DMA((FIELDS + 8,)),
-            pltpu.SemaphoreType.DMA((8, 8)),
-            pltpu.SemaphoreType.DMA((8, 8)),
+            pltpu.SemaphoreType.DMA((6, 8)),
+            pltpu.SemaphoreType.DMA((6, 8)),
         ],
         compiler_params=pltpu.CompilerParams(collective_id=0, has_side_effects=True, vmem_limit_bytes=62 << 20),
     )(pot_temp, tracer, wind_u, wind_v, vert_w, geopot, elem_mass.T, deriv_x, deriv_y, col_inverse, element_cell, rows, lanes)

time: 25 us -> 22.8 us (0.912)
  the two profiles are of different devices: /device:TPU:0 before, /device:TPU:1 now
where the time goes in v4:
time: 22.8 us; the launch traced here: 22.4 us
  Pallas kernels  21.8 us (96%)
  between operations  0.64 us (3%)
    pallas_call x1, Pallas kernels, per_device(): pl.pallas_call(step_kernel, out_shape=pltpu.VMEM((FIELDS,) + shape, F32),...  20.6 us
    pallas_call x1, Pallas kernels, per_device(): pl.pallas_call(store_kernel, out_shape=[result] * FIELDS, in_specs=[vmem]...  1.19 us

profile of v4, /device:TPU:1, one launch (start us, length us, event | category | flops | bytes accessed | tf_op | source)
XLA Modules:
  0.0 22.4 jit_solution(5460354525576267337)
XLA Ops:
  0.6 20.6 %shard_map.172.fields = f32[6,32,16,128]{3,2,1,0:T(8,128)S(1)} custom-call(f32[32,16,128]{2,1,0:T(8,128)} %pot_in.1, f32[32,16,128]{2,1,0:T(8,128)} %tracer_in.1, f32[32,16,128]{2,1,0:T(8,128)} %u_in.1, f32[32,16,128]{2,1,0:T(8,128)} %v_in.1, f32[32,16,128]{2,1,0:T(8,128)} %w_in.1, f32[32,16,128]{2,1,0:T(8,128)} %geo_in.1, f32[16,32]{1,0:T(8,128)} %bitcast.1, ...), custom_call_target="tpu_custom_call" | custom-call | tf_op jit(solution)/shard_map/pallas_call | solution.py:517
  21.2 1.2 %shard_map.173 = (f32[32,16,128]{2,1,0:T(8,128)}, f32[32,16,128]{2,1,0:T(8,128)}, f32[32,16,128]{2,1,0:T(8,128)}, f32[32,16,128]{2,1,0:T(8,128)}, f32[32,16,128]{2,1,0:T(8,128)}, /*index=5*/f32[32,16,128]{2,1,0:T(8,128)}) custom-call(f32[6,32,16,128]{3,2,1,0:T(8,128)S(1)} %shard_map.172.fields), custom_call_target="tpu_custom_call" | custom-call | tf_op jit(solution)/shard_map/pallas_call | solution.py:557

commit v5 on v4

--- a/solution.py
+++ b/solution.py
@@ -57,7 +57,7 @@
 )
 SIDE_LINES = ((0, 25, 0, 16), (32, 25, 12, 16), (64, 13, 0, 1), (88, 13, 384, 1))
 CORNER_LINES = LINES[4:]
-PLACE, KNOWN, LINE, UNIQUE, EDGE, LATE, CLOSE, SLOT = range(8)
+PLACE, KNOWN, LINE, UNIQUE, CLOSE, SLOT, FACING = range(7)
 
 
 def rim_tables():
@@ -81,13 +81,12 @@
         ny = node[theirs] // PITCH + 3 * TY * SIDES[k][0]
         nx = node[theirs] % PITCH + 3 * TX * SIDES[k][1]
         place[mine[known]] = ((ny + 8) * 64 + nx + 8)[known]
+    facing = np.array(OPPOSITE)[slot.astype(int)]
     corner = np.zeros(RIM)
     corner[[0, 24, 40, 64, 80, 92, 112, 124]] = 1
     unique = line * (slot < 4) * np.where(slot < 2, 1, 1 - corner)
-    edge = line * (slot < 4) * (1 - corner)
-    late = np.where(slot < 4, corner, node >= 0)
     rows = np.zeros((RIM, LEV))
-    for column, table in enumerate((place, node >= 0, line, unique, edge, late, close, slot)):
+    for column, table in enumerate((place, node >= 0, line, unique, close, slot, facing)):
         rows[:, column] = table
     lanes = np.full((3, 8, 2 * LEV), -9000.0)
     lanes[:, :, :RIM] = np.stack([lane_node, place, slot])[:, None]
@@ -184,7 +183,7 @@
     out,
     mass_in, dx_in, dy_in, col_in, cells, cells_row, row_tab, lane_tab,
     xin, xc, mid, s1, s2, s3, s4, mgrid, rinv, mcol, kmat, inv,
-    send1, recv0, recv1, recv_vert, local, away, foreign, rim_inv,
+    send1, recv0, recv1, recv_vert, local, packed, away, foreign, rim_inv,
     load_sem, send_sem, recv_sem,
 ):
     row = lax.axis_index("sfc")
@@ -242,7 +241,7 @@
         inv[c] = slot
         return carry
 
-    lax.fori_loop(0, TX * TY, invert, 0)
+    lax.fori_loop(0, TX * TY, invert, 0, unroll=True)
 
     dx = dx_in[...]
     dy = dy_in[...]
@@ -278,6 +277,20 @@
 
     lax.fori_loop(0, TY, mass_strip, 0, unroll=True)
     gather_rim(mgrid, send1, (LINES, NEAR, FAR), range(1), 1)
+    lap = exact(dx, dx) + exact(dy, dy)
+    lap_blk = block_diag(lap, 3 * STRIP)
+    spread3 = onehot(node_point(iota((STRIP, 3 * STRIP), 1) % STRIP, iota((STRIP, 3 * STRIP), 0)))
+    lap_nodes = exact(block_diag(lap, STRIP), spread3)
+
+    def matrix_strip(ey, carry):
+        strip_mass = mcol[pl.ds(pl.multiple_of(STRIP * ey, STRIP), STRIP)]
+        wide = jnp.concatenate([strip_mass, strip_mass[:, :STRIP]], axis=1)
+        kmat[0, ey] = weight3(mm(gather2, stack2(wide * lap_blk)))
+        kmat[1, ey] = weight3(mm(gather2, stack2(wide * lap_nodes)))
+        return carry
+
+    lax.fori_loop(0, TY, matrix_strip, 0, unroll=True)
+
     for load in loads:
         load.wait()
 
@@ -286,11 +299,13 @@
 
     def tend_strip(ey, carry):
         points = pl.ds(pl.multiple_of(STRIP * ey, STRIP), STRIP)
-        for ex in range(TX):
-            slot = inv[TX * ey + ex]
-            for k in range(FIELDS):
-                xc[k, TX * ey + ex] = xin[k, slot]
-        x = strip_of(xc, ey, range(FIELDS))
+        fields = []
+        for k in range(FIELDS):
+            parts = [xin[k, inv[TX * ey + ex]] for ex in range(TX)]
+            for ex in range(TX):
+                xc[k, TX * ey + ex] = parts[ex]
+            fields.append(jnp.concatenate(parts, axis=0))
+        x = jnp.concatenate(fields, axis=1)
         slopes = mm(deriv3, stack3(x[:, : 4 * LEV]))
         sx = slopes[:STRIP]
         sy = slopes[STRIP:]
@@ -348,20 +363,6 @@
             for n, (ey, ex) in enumerate(part):
                 mid[TX * ey + ex] = phi[16 * n : 16 * n + 16]
 
-    lap = exact(dx, dx) + exact(dy, dy)
-    lap_blk = block_diag(lap, 3 * STRIP)
-    spread3 = onehot(node_point(iota((STRIP, 3 * STRIP), 1) % STRIP, iota((STRIP, 3 * STRIP), 0)))
-    lap_nodes = exact(block_diag(lap, STRIP), spread3)
-
-    def matrix_strip(ey, carry):
-        strip_mass = mcol[pl.ds(pl.multiple_of(STRIP * ey, STRIP), STRIP)]
-        wide = jnp.concatenate([strip_mass, strip_mass[:, :STRIP]], axis=1)
-        kmat[0, ey] = weight3(mm(gather2, stack2(wide * lap_blk)))
-        kmat[1, ey] = weight3(mm(gather2, stack2(wide * lap_nodes)))
-        return carry
-
-    lax.fori_loop(0, TY, matrix_strip, 0, unroll=True)
-
     def column(kind):
         return row_tab[:, kind : kind + 1]
 
@@ -391,7 +392,15 @@
 
     lax.fori_loop(0, TY, first_strip, 0, unroll=True)
     gather_rim(s2, local, (LINES, NEAR), range(6))
-    near_copies = exchange(3, local, away, range(8), OFFSET, NEAR_COUNT, (0, 6))
+    facing = column(FACING) == lane_tab[2][0:1]
+
+    def fold(blocks):
+        both = jnp.where(facing, lanes_of(local, blocks), 0.0)
+        return both[:, :LEV] + both[:, LEV:]
+
+    packed[0:4] = local[0:4]
+    packed[4] = fold(range(4, 6))
+    near_copies = exchange(3, packed, away, range(8), OFFSET, NEAR_COUNT, (0, 5))
 
     def second_strip(ey, carry):
         start = pl.multiple_of(48 * ey, 16)
@@ -401,7 +410,9 @@
 
     lax.fori_loop(0, TY, second_strip, 0, unroll=True)
     gather_rim(s3, local, (LINES,), range(6), 6)
-    far_copies = exchange(5, local, away, range(8), OFFSET, LINE_COUNT, (6, 6))
+    packed[5:9] = local[6:10]
+    packed[9] = fold(range(10, 12))
+    far_copies = exchange(5, packed, away, range(8), OFFSET, LINE_COUNT, (5, 5))
 
     own_weight = halves(lanes_of(local, range(4, 6))[:, :RIM])
     again_weight = halves(lanes_of(s3, range(4, 6))[:, :RIM])
@@ -418,8 +429,10 @@
     own_block = column(SLOT) == lane_tab[2][0:1]
     close = column(CLOSE) > 0.0
 
+    for copy in vert_copies + line_copies + near_copies + far_copies:
+        copy.wait_send()
     for copy in vert_copies:
-        copy.wait()
+        copy.wait_recv()
     add_rim(mgrid, recv_vert.at[pl.ds(1, 1)], range(1))
     rinv[0] = reciprocal(mgrid[0])
     for row, rows, start, stride in LINES:
@@ -430,7 +443,7 @@
     )
 
     for copy in line_copies:
-        copy.wait()
+        copy.wait_recv()
     side_lines = spread_rows(
         [lanes_of(recv0, range(2, 6))[first : first + rows] for first, rows in zip(TURN_OFFSET, TURN_ROWS)]
         + [jnp.zeros((16, 4 * LEV), F32)] * 4
@@ -464,16 +477,16 @@
 
     inverse = rim_inv[...]
     for copy in near_copies:
-        copy.wait()
-    rim_matrix = jnp.where(own_block & close, lanes_of(away, range(4, 6)), 0.0)
+        copy.wait_recv()
+    rim_matrix = jnp.where(own_block & close, lanes_of(away, (4, 4)), 0.0)
     first_turn = jnp.where(close, lanes_of(away, range(4)), 0.0) + mm3(rim_matrix, rim_state)
     rim_next = merge(first_turn) * wide(inverse) + own_rim
     outside = mm3(rim_matrix, rim_next)
     inner = mm3(inner_weight, swap_sides(rim_next * unique))
     for copy in far_copies:
-        copy.wait()
-    rim_matrix2 = jnp.where(own_block & (line > 0.0), lanes_of(away, range(10, 12)), 0.0)
-    outside = outside + jnp.where(line > 0.0, lanes_of(away, range(6, 10)), 0.0) + mm3(rim_matrix2, rim_state)
+        copy.wait_recv()
+    rim_matrix2 = jnp.where(own_block & (line > 0.0), lanes_of(away, (9, 9)), 0.0)
+    outside = outside + jnp.where(line > 0.0, lanes_of(away, range(5, 9)), 0.0) + mm3(rim_matrix2, rim_state)
     for k in range(4):
         foreign[k] = outside[:, k * LEV : (k + 1) * LEV]
         s4[k] = s4[k] + inner[:, k * LEV : (k + 1) * LEV]
@@ -543,7 +556,7 @@
         ]
         + [pltpu.VMEM((6, RIM, LEV), F32), pltpu.VMEM((6, TURN_RIM, LEV), F32), pltpu.VMEM((6, RIM, LEV), F32)]
         + [pltpu.VMEM((2, RIM, LEV), F32)]
-        + [pltpu.VMEM((blocks, RIM, LEV), F32) for blocks in (12, 12, 4)]
+        + [pltpu.VMEM((blocks, RIM, LEV), F32) for blocks in (12, 10, 10, 4)]
         + [
             pltpu.VMEM((RIM, LEV), F32),
             pltpu.SemaphoreType.DMA((FIELDS + 8,)),

time: 22.8 us -> 22.1 us (0.969)
  Pallas kernels: 21.8 us -> 21.1 us
    pallas_call x1, Pallas kernels: 20.6 us -> 20 us  [per_device(): pl.pallas_call(step_kernel, out_shape=pltpu.VMEM((FIELDS,) + shape, F32),...]
where the time goes in v5:
time: 22.1 us; the launch traced here: 21.8 us
  Pallas kernels  21.1 us (95%)
  between operations  0.64 us (3%)
    pallas_call x1, Pallas kernels, per_device(): pl.pallas_call(step_kernel, out_shape=pltpu.VMEM((FIELDS,) + shape, F32),...  20 us
    pallas_call x1, Pallas kernels, per_device(): pl.pallas_call(store_kernel, out_shape=[result] * FIELDS, in_specs=[vmem]...  1.19 us

profile of v5, /device:TPU:1, one launch (start us, length us, event | category | flops | bytes accessed | tf_op | source)
XLA Modules:
  0.0 21.8 jit_solution(8136433826886137006)
XLA Ops:
  0.6 20.0 %shard_map.172.fields = f32[6,32,16,128]{3,2,1,0:T(8,128)S(1)} custom-call(f32[32,16,128]{2,1,0:T(8,128)} %pot_in.1, f32[32,16,128]{2,1,0:T(8,128)} %tracer_in.1, f32[32,16,128]{2,1,0:T(8,128)} %u_in.1, f32[32,16,128]{2,1,0:T(8,128)} %v_in.1, f32[32,16,128]{2,1,0:T(8,128)} %w_in.1, f32[32,16,128]{2,1,0:T(8,128)} %geo_in.1, f32[16,32]{1,0:T(8,128)} %bitcast.1, ...), custom_call_target="tpu_custom_call" | custom-call | tf_op jit(solution)/shard_map/pallas_call | solution.py:530
  20.6 1.2 %shard_map.173 = (f32[32,16,128]{2,1,0:T(8,128)}, f32[32,16,128]{2,1,0:T(8,128)}, f32[32,16,128]{2,1,0:T(8,128)}, f32[32,16,128]{2,1,0:T(8,128)}, f32[32,16,128]{2,1,0:T(8,128)}, /*index=5*/f32[32,16,128]{2,1,0:T(8,128)}) custom-call(f32[6,32,16,128]{3,2,1,0:T(8,128)S(1)} %shard_map.172.fields), custom_call_target="tpu_custom_call" | custom-call | tf_op jit(solution)/shard_map/pallas_call | solution.py:570

commit v6 on v5

--- a/solution.py
+++ b/solution.py
@@ -183,7 +183,7 @@
     out,
     mass_in, dx_in, dy_in, col_in, cells, cells_row, row_tab, lane_tab,
     xin, xc, mid, s1, s2, s3, s4, mgrid, rinv, mcol, kmat, inv,
-    send1, recv0, recv1, recv_vert, local, packed, away, foreign, rim_inv,
+    send1, recv0, recv1, recv_vert, local, away, foreign, rim_inv,
     load_sem, send_sem, recv_sem,
 ):
     row = lax.axis_index("sfc")
@@ -330,9 +330,9 @@
     pl.semaphore_wait(barrier, 8)
     far_start = [first + n for first, n in zip(OFFSET, LINE_COUNT)]
     far_count = [n - m for m, n in zip(LINE_COUNT, FULL_COUNT)]
-    vert_copies = exchange(4, send1, recv_vert, range(8), OFFSET, LINE_COUNT, (0, 2))
-    line_copies = exchange(0, send1, recv0, DIRECT, OFFSET, LINE_COUNT, (2, 4), TURN_OFFSET)
-    line_copies += exchange(1, send1, recv1, DIAGONAL, OFFSET, FULL_COUNT, (1, 5))
+    vert_copies = exchange(4, send1, recv_vert, (2, 3, 4, 5, 6, 7, 0, 1), OFFSET, LINE_COUNT, (0, 2))
+    line_copies = exchange(1, send1, recv1, DIAGONAL, OFFSET, FULL_COUNT, (1, 5))
+    line_copies += exchange(0, send1, recv0, DIRECT, OFFSET, LINE_COUNT, (2, 4), TURN_OFFSET)
     line_copies += exchange(2, send1, recv1, DIRECT, far_start, far_count, (1, 5))
 
     col_high, col_low = halves(col_in[...])
@@ -391,16 +391,16 @@
         return carry
 
     lax.fori_loop(0, TY, first_strip, 0, unroll=True)
-    gather_rim(s2, local, (LINES, NEAR), range(6))
+    gather_rim(s2, local, (LINES, NEAR), range(4))
+    gather_rim(s2, local, (LINES, NEAR), range(4, 6), 10)
     facing = column(FACING) == lane_tab[2][0:1]
 
     def fold(blocks):
         both = jnp.where(facing, lanes_of(local, blocks), 0.0)
         return both[:, :LEV] + both[:, LEV:]
 
-    packed[0:4] = local[0:4]
-    packed[4] = fold(range(4, 6))
-    near_copies = exchange(3, packed, away, range(8), OFFSET, NEAR_COUNT, (0, 5))
+    local[4] = fold(range(10, 12))
+    near_copies = exchange(3, local, away, (2, 3, 4, 5, 6, 7, 0, 1), OFFSET, NEAR_COUNT, (0, 5))
 
     def second_strip(ey, carry):
         start = pl.multiple_of(48 * ey, 16)
@@ -409,12 +409,12 @@
         return carry
 
     lax.fori_loop(0, TY, second_strip, 0, unroll=True)
-    gather_rim(s3, local, (LINES,), range(6), 6)
-    packed[5:9] = local[6:10]
-    packed[9] = fold(range(10, 12))
-    far_copies = exchange(5, packed, away, range(8), OFFSET, LINE_COUNT, (5, 5))
-
-    own_weight = halves(lanes_of(local, range(4, 6))[:, :RIM])
+    gather_rim(s3, local, (LINES,), range(4), 5)
+    gather_rim(s3, local, (LINES,), range(4, 6), 12)
+    local[9] = fold(range(12, 14))
+    far_copies = exchange(5, local, away, (2, 3, 4, 5, 6, 7, 0, 1), OFFSET, LINE_COUNT, (5, 5))
+
+    own_weight = halves(lanes_of(local, range(10, 12))[:, :RIM])
     again_weight = halves(lanes_of(s3, range(4, 6))[:, :RIM])
     inner_weight = halves(lanes_of(s2, range(4, 6))[:, :RIM])
     newton([(ey, ex) for ey in range(1, TY - 1) for ex in (1, 2)], 1)
@@ -556,7 +556,7 @@
         ]
         + [pltpu.VMEM((6, RIM, LEV), F32), pltpu.VMEM((6, TURN_RIM, LEV), F32), pltpu.VMEM((6, RIM, LEV), F32)]
         + [pltpu.VMEM((2, RIM, LEV), F32)]
-        + [pltpu.VMEM((blocks, RIM, LEV), F32) for blocks in (12, 10, 10, 4)]
+        + [pltpu.VMEM((blocks, RIM, LEV), F32) for blocks in (14, 10, 4)]
         + [
             pltpu.VMEM((RIM, LEV), F32),
             pltpu.SemaphoreType.DMA((FIELDS + 8,)),

time: 22.1 us -> 21.5 us (0.973)
  Pallas kernels: 21.1 us -> 20.6 us
    pallas_call x1, Pallas kernels: 20 us -> 19.4 us  [per_device(): pl.pallas_call(step_kernel, out_shape=pltpu.VMEM((FIELDS,) + shape, F32),...]
where the time goes in v6:
time: 21.5 us; the launch traced here: 21.3 us
  Pallas kernels  20.6 us (96%)
  between operations  0.64 us (3%)
    pallas_call x1, Pallas kernels, per_device(): pl.pallas_call(step_kernel, out_shape=pltpu.VMEM((FIELDS,) + shape, F32),...  19.4 us
    pallas_call x1, Pallas kernels, per_device(): pl.pallas_call(store_kernel, out_shape=[result] * FIELDS, in_specs=[vmem]...  1.19 us

profile of v6, /device:TPU:1, one launch (start us, length us, event | category | flops | bytes accessed | tf_op | source)
XLA Modules:
  0.0 21.3 jit_solution(6899242303475557984)
XLA Ops:
  0.6 19.4 %shard_map.172.fields = f32[6,32,16,128]{3,2,1,0:T(8,128)S(1)} custom-call(f32[32,16,128]{2,1,0:T(8,128)} %pot_in.1, f32[32,16,128]{2,1,0:T(8,128)} %tracer_in.1, f32[32,16,128]{2,1,0:T(8,128)} %u_in.1, f32[32,16,128]{2,1,0:T(8,128)} %v_in.1, f32[32,16,128]{2,1,0:T(8,128)} %w_in.1, f32[32,16,128]{2,1,0:T(8,128)} %geo_in.1, f32[16,32]{1,0:T(8,128)} %bitcast.1, ...), custom_call_target="tpu_custom_call" | custom-call | tf_op jit(solution)/shard_map/pallas_call | solution.py:530
  20.1 1.2 %shard_map.173 = (f32[32,16,128]{2,1,0:T(8,128)}, f32[32,16,128]{2,1,0:T(8,128)}, f32[32,16,128]{2,1,0:T(8,128)}, f32[32,16,128]{2,1,0:T(8,128)}, f32[32,16,128]{2,1,0:T(8,128)}, /*index=5*/f32[32,16,128]{2,1,0:T(8,128)}) custom-call(f32[6,32,16,128]{3,2,1,0:T(8,128)S(1)} %shard_map.172.fields), custom_call_target="tpu_custom_call" | custom-call | tf_op jit(solution)/shard_map/pallas_call | solution.py:570
